TPU v7x, 32 devices: a whole 2x2x4 slice. The times are simulated.
32 devices in a mesh: batch: 2 (over core), ctx: 16 (over z, y, x).
Axes of the slice: x: 2, y: 2, z: 4, core: 2. Of those that a mesh axis runs over, the one named last changes fastest.
Arguments:
- inputs: bfloat16 [2, 2, 1536, 1024], P(None, 'batch', 'ctx'), may hold values from -6 to 6
- cotangent: bfloat16 [2, 2, 1536, 1024], P(None, 'batch', 'ctx'), may hold values from -6 to 6
- routes: int32 [2, 2, 1536, 8], P(None, 'batch'), may hold values from 0 to 15, all different within a row
- segments: int32 [2, 2, 1536], P(None, 'batch'), may hold values from 0 to 5, as said below
- gains: float32 [2, 1024], P(None, ('batch', 'ctx')), may hold values from 0.5 to 1.5
- gains_first: float32 [2, 1024], P(None, ('batch', 'ctx')), may hold values from -80 to 80
- gains_second: float32 [2, 1024], P(None, ('batch', 'ctx')), may hold values from 356.352 to 5836.8
- w_query: float32 [1024, 1024], P(('batch', 'ctx')), may hold values from -0.1875 to 0.1875
- query_first: float32 [1024, 1024], P(('batch', 'ctx')), may hold values from -80 to 80
- query_second: float32 [1024, 1024], P(('batch', 'ctx')), may hold values from 356.352 to 5836.8
- w_keyvalue: float32 [1024, 1024], P(('batch', 'ctx')), may hold values from -0.1875 to 0.1875
- keyvalue_first: float32 [1024, 1024], P(('batch', 'ctx')), may hold values from -80 to 80
- keyvalue_second: float32 [1024, 1024], P(('batch', 'ctx')), may hold values from 356.352 to 5836.8
- w_out: float32 [1024, 1024], P(('batch', 'ctx')), may hold values from -1.5 to 1.5
- out_first: float32 [1024, 1024], P(('batch', 'ctx')), may hold values from -5 to 5
- out_second: float32 [1024, 1024], P(('batch', 'ctx')), may hold values from 1.59744 to 25.8048
- w_router: float32 [1024, 16], P(('batch', 'ctx')), may hold values from -0.09375 to 0.09375
- router_first: float32 [1024, 16], P(('batch', 'ctx')), may hold values from -384 to 384
- router_second: float32 [1024, 16], P(('batch', 'ctx')), may hold values from 7802.88 to 126566.4
- w_gate_up: float32 [16, 1024, 1024], P(None, ('batch', 'ctx')), may hold values from -0.1875 to 0.1875
- gate_up_first: float32 [16, 1024, 1024], P(None, ('batch', 'ctx')), may hold values from -16 to 16
- gate_up_second: float32 [16, 1024, 1024], P(None, ('batch', 'ctx')), may hold values from 19.6608 to 313.344
- w_down: float32 [16, 1024, 512], P(None, ('batch', 'ctx')), may hold values from -1 to 1
- down_first: float32 [16, 1024, 512], P(None, ('batch', 'ctx')), may hold values from -3 to 3
- down_second: float32 [16, 1024, 512], P(None, ('batch', 'ctx')), may hold values from 0.577536 to 9.216
Outputs:
- outputs: bfloat16 [2, 2, 1536, 1024], P(None, 'batch', 'ctx')
- input_grad: float32 [2, 2, 1536, 1024], P(None, 'batch', 'ctx')
- gains_moment: float32 [2, 1024], P(None, ('batch', 'ctx'))
- gains_square: float32 [2, 1024], P(None, ('batch', 'ctx'))
- gains_new: float32 [2, 1024], P(None, ('batch', 'ctx'))
- query_moment: float32 [1024, 1024], P(('batch', 'ctx'))
- query_square: float32 [1024, 1024], P(('batch', 'ctx'))
- query_new: float32 [1024, 1024], P(('batch', 'ctx'))
- keyvalue_moment: float32 [1024, 1024], P(('batch', 'ctx'))
- keyvalue_square: float32 [1024, 1024], P(('batch', 'ctx'))
- keyvalue_new: float32 [1024, 1024], P(('batch', 'ctx'))
- out_moment: float32 [1024, 1024], P(('batch', 'ctx'))
- out_square: float32 [1024, 1024], P(('batch', 'ctx'))
- out_new: float32 [1024, 1024], P(('batch', 'ctx'))
- router_moment: float32 [1024, 16], P(('batch', 'ctx'))
- router_square: float32 [1024, 16], P(('batch', 'ctx'))
- router_new: float32 [1024, 16], P(('batch', 'ctx'))
- gate_up_moment: float32 [16, 1024, 1024], P(None, ('batch', 'ctx'))
- gate_up_square: float32 [16, 1024, 1024], P(None, ('batch', 'ctx'))
- gate_up_new: float32 [16, 1024, 1024], P(None, ('batch', 'ctx'))
- down_moment: float32 [16, 1024, 512], P(None, ('batch', 'ctx'))
- down_square: float32 [16, 1024, 512], P(None, ('batch', 'ctx'))
- down_new: float32 [16, 1024, 512], P(None, ('batch', 'ctx'))
Inputs may be any that keep to these rules, and one draw needn't show every extreme that they name: `routes`: each token names 8 different experts. `segments`: within a sequence the numbers never fall and start at 0. For each index of the second dimension, one of the 2 micro-batches (first dimension), drawn from the seed, holds a single-document sequence; the other holds 6 documents.
All inputs are finite; a program needn't handle non-finite values.
Results may differ from a plain program's by a relative error of at most 0.03.
Values may be sent and summed in bfloat16 or wider, within the bound.
A program may use at most 384 MiB of HBM per device.

v0:
```python
import math

import jax
import jax.numpy as jnp
from jax import lax
from jax.sharding import PartitionSpec as P

HEADS = 16
KV_HEADS = 8
HEAD_DIM = 64
FF = 512
EXPERTS = 16
STEP = 10


EPS_NORM = 1e-06
EPS_ADAM = 1e-08
BETA_ONE = 0.9
BETA_TWO = 0.95
MASKED = -1e30
ROPE_BASE = 10000.0
RATES = (1.0, 0.04, 0.1, 1.5, 0.02, 0.1, 0.2)
DECAYS = (0.0, 0.1, 0.1, 0.1, 0.1, 0.1, 0.1)
HIGHEST = lax.Precision.HIGHEST


def rope_tables(positions):
    half_width = HEAD_DIM // 2
    frequency = ROPE_BASE ** (-(jnp.arange(half_width, dtype=jnp.float32) * 2.0) / HEAD_DIM)
    angles = positions.astype(jnp.float32)[:, None] * frequency[None, :]
    return (jnp.cos(angles), jnp.sin(angles))


def rotate(values, cosine_table, sine_table):
    half_width = values.shape[-1] // 2
    first_half = values[..., :half_width]
    second_half = values[..., half_width:]
    cos_rows = cosine_table[:, None, :]
    sin_rows = sine_table[:, None, :]
    return jnp.concatenate(
        [
            first_half * cos_rows - second_half * sin_rows,
            second_half * cos_rows + first_half * sin_rows,
        ],
        axis=-1,
    )


def prepare_blocks(shard_rows):
    total_rows = shard_rows.shape[0]
    step_rows = math.gcd(total_rows, 512)
    blocks = shard_rows.reshape(total_rows // step_rows, step_rows, shard_rows.shape[1])
    offsets = jnp.arange(total_rows // step_rows, dtype=jnp.int32) * step_rows
    return (blocks, offsets, step_rows)


def block_scores(grouped, block_rows, key_start, step_rows, query_seg, query_pos, segment_row):
    kv_width = KV_HEADS * HEAD_DIM
    key_rows = block_rows[:, :kv_width].reshape(step_rows, KV_HEADS, HEAD_DIM)
    value_rows = block_rows[:, kv_width:].reshape(step_rows, KV_HEADS, HEAD_DIM)
    key_seg = lax.dynamic_slice_in_dim(segment_row, key_start, step_rows)
    key_pos = key_start + jnp.arange(step_rows, dtype=jnp.int32)
    allowed = ((query_seg[:, None] == key_seg[None, :]) & (query_pos[:, None] >= key_pos[None, :]))[
        None, None
    ]
    scores = jnp.einsum(
        "cgrd,kgd->grck", grouped, key_rows, preferred_element_type=jnp.float32
    ) * HEAD_DIM ** (-0.5)
    return (key_rows, value_rows, allowed, jnp.where(allowed, scores, MASKED))


def fold_forward(running, shard_rows, grouped, query_seg, query_pos, segment_row, limit):
    blocks, offsets, step_rows = prepare_blocks(shard_rows)

    def visit(current, block_pair):
        block_rows, offset = block_pair

        def attend(inner):
            maxima, totals, accumulated = inner
            key_rows, value_rows, allowed, scores = block_scores(
                grouped, block_rows, offset, step_rows, query_seg, query_pos, segment_row
            )
            new_max = jnp.maximum(maxima, jnp.max(scores, axis=-1))
            fading = jnp.exp(maxima - new_max)
            block_weights = jnp.where(allowed, jnp.exp(scores - new_max[..., None]), 0.0)
            totals = totals * fading + jnp.sum(block_weights, axis=-1)
            update = jnp.einsum(
                "grck,kgd->cgrd",
                block_weights.astype(jnp.bfloat16),
                value_rows,
                preferred_element_type=jnp.float32,
            )
            accumulated = accumulated * jnp.transpose(fading, (2, 0, 1))[..., None] + update
            return (new_max, totals, accumulated)

        return (lax.cond(offset < limit, attend, lambda inner: inner, current), None)

    running, unused = lax.scan(visit, running, (blocks, offsets))
    return running


def fold_backward(
    running,
    shard_rows,
    grouped,
    grad_grouped,
    log_totals,
    deltas,
    query_seg,
    query_pos,
    segment_row,
    limit,
):
    blocks, offsets, step_rows = prepare_blocks(shard_rows)
    kv_width = KV_HEADS * HEAD_DIM
    factor = HEAD_DIM ** (-0.5)

    def visit(current, block_pair):
        block_rows, offset = block_pair

        def attend(inner):
            grad_query, grad_keys = inner
            key_rows, value_rows, allowed, scores = block_scores(
                grouped, block_rows, offset, step_rows, query_seg, query_pos, segment_row
            )
            block_weights = jnp.where(allowed, jnp.exp(scores - log_totals[..., None]), 0.0)
            grad_weights = jnp.einsum(
                "cgrd,kgd->grck", grad_grouped, value_rows, preferred_element_type=jnp.float32
            )
            grad_scores = (block_weights * (grad_weights - deltas[..., None])).astype(jnp.bfloat16)
            grad_query = (
                grad_query
                + jnp.einsum(
                    "grck,kgd->cgrd", grad_scores, key_rows, preferred_element_type=jnp.float32
                )
                * factor
            )
            key_part = (
                jnp.einsum(
                    "grck,cgrd->kgd", grad_scores, grouped, preferred_element_type=jnp.float32
                )
                * factor
            )
            value_part = jnp.einsum(
                "grck,cgrd->kgd",
                block_weights.astype(jnp.bfloat16),
                grad_grouped,
                preferred_element_type=jnp.float32,
            )
            block_grad = jnp.concatenate(
                [key_part.reshape(step_rows, kv_width), value_part.reshape(step_rows, kv_width)],
                axis=1,
            )
            previous = lax.dynamic_slice_in_dim(grad_keys, offset, step_rows, 0)
            grad_keys = lax.dynamic_update_slice_in_dim(grad_keys, previous + block_grad, offset, 0)
            return (grad_query, grad_keys)

        return (lax.cond(offset < limit, attend, lambda inner: inner, current), None)

    running, unused = lax.scan(visit, running, (blocks, offsets))
    return running


def attention_forward(dense_set, tokens, segment_row, cosine_table, sine_table, anchor):
    gains_low, query_low, keyvalue_low, out_low, router_low = dense_set
    kv_width = KV_HEADS * HEAD_DIM
    group_size = HEADS // KV_HEADS
    span_rows = tokens.shape[0]
    inv_first = lax.rsqrt(jnp.mean(tokens * tokens, axis=-1, keepdims=True) + EPS_NORM)
    unit_first = tokens * inv_first
    normed = (unit_first * gains_low[0].astype(jnp.float32)).astype(jnp.bfloat16)
    query_raw = jnp.dot(normed, query_low, preferred_element_type=jnp.float32)
    keyvalue_raw = jnp.dot(normed, keyvalue_low, preferred_element_type=jnp.float32)
    queries = rotate(
        query_raw.reshape(span_rows, HEADS, HEAD_DIM), cosine_table, sine_table
    ).astype(jnp.bfloat16)
    key_rows = rotate(
        keyvalue_raw[:, :kv_width].reshape(span_rows, KV_HEADS, HEAD_DIM), cosine_table, sine_table
    ).astype(jnp.bfloat16)
    shipped = jnp.concatenate(
        [key_rows.reshape(span_rows, kv_width), keyvalue_raw[:, kv_width:].astype(jnp.bfloat16)],
        axis=1,
    )
    grouped = queries.reshape(span_rows, KV_HEADS, group_size, HEAD_DIM)
    query_seg = lax.dynamic_slice_in_dim(segment_row, anchor, span_rows)
    query_pos = anchor + jnp.arange(span_rows, dtype=jnp.int32)
    limit = anchor + span_rows
    start_state = (
        jnp.full((KV_HEADS, group_size, span_rows), MASKED, jnp.float32),
        jnp.zeros((KV_HEADS, group_size, span_rows), jnp.float32),
        jnp.zeros((span_rows, KV_HEADS, group_size, HEAD_DIM), jnp.float32),
    )
    maxima, totals, accumulated = fold_forward(
        start_state,
        lax.all_gather(shipped, "ctx", axis=0, tiled=True),
        grouped,
        query_seg,
        query_pos,
        segment_row,
        limit,
    )
    attended = (accumulated / jnp.transpose(totals, (2, 0, 1))[..., None]).reshape(
        span_rows, HEADS * HEAD_DIM
    )
    log_totals = maxima + jnp.log(totals)
    attended_low = attended.astype(jnp.bfloat16)
    branch = jnp.einsum("ch,dh->cd", attended_low, out_low, preferred_element_type=jnp.float32)
    middle = tokens + branch
    inv_second = lax.rsqrt(jnp.mean(middle * middle, axis=-1, keepdims=True) + EPS_NORM)
    unit_second = middle * inv_second
    normed_ffn = (unit_second * gains_low[1].astype(jnp.float32)).astype(jnp.bfloat16)
    saved = (
        unit_first,
        inv_first,
        normed,
        grouped,
        shipped,
        attended,
        attended_low,
        log_totals,
        query_seg,
        query_pos,
        unit_second,
        inv_second,
    )
    return (middle, normed_ffn, saved)


def route_gates(normed_rows, router_low, route_rows):
    logits = jnp.dot(normed_rows, router_low, preferred_element_type=jnp.float32)
    selection = (
        route_rows[:, :, None] == jnp.arange(EXPERTS, dtype=jnp.int32)[None, None, :]
    ).astype(jnp.float32)
    chosen = jnp.sum(selection * logits[:, None, :], axis=-1)
    shares = jax.nn.softmax(chosen, axis=-1)
    gate_table = jnp.sum(shares[:, :, None] * selection, axis=1)
    return (selection, shares, gate_table)


def swiglu_back(grad_active, gate_part, up_part):
    sigmoid_gate = jax.nn.sigmoid(gate_part)
    grad_gate = grad_active * up_part * sigmoid_gate * (1.0 + gate_part * (1.0 - sigmoid_gate))
    grad_up = grad_active * gate_part * sigmoid_gate
    return (grad_gate, grad_up)


def experts_forward(normed_ffn, gate_table, gate_up_low, down_low):
    gate_and_up = jnp.einsum(
        "cd,edf->cef", normed_ffn, gate_up_low, preferred_element_type=jnp.float32
    )
    active = jax.nn.silu(gate_and_up[..., :FF]) * gate_and_up[..., FF:]
    scaled = (gate_table[:, :, None] * active).astype(jnp.bfloat16)
    expert_sum = jnp.einsum("cef,edf->cd", scaled, down_low, preferred_element_type=jnp.float32)
    return (expert_sum, (gate_and_up, active, scaled))


def experts_backward(grad_result, normed_ffn, gate_table, kept_rows, gate_up_low, down_low, sums):
    gate_and_up, active, scaled = kept_rows
    sum_gate_up, sum_down = sums
    sum_down = sum_down + jnp.einsum(
        "cef,cd->edf", scaled, grad_result, preferred_element_type=jnp.float32
    )
    grad_scaled = jnp.einsum(
        "cd,edf->cef", grad_result, down_low, preferred_element_type=jnp.float32
    )
    grad_gate_table = jnp.sum(grad_scaled * active, axis=-1)
    grad_gate, grad_up = swiglu_back(
        gate_table[:, :, None] * grad_scaled, gate_and_up[..., :FF], gate_and_up[..., FF:]
    )
    grad_both = jnp.concatenate([grad_gate, grad_up], axis=-1).astype(jnp.bfloat16)
    sum_gate_up = sum_gate_up + jnp.einsum(
        "cd,cef->edf", normed_ffn, grad_both, preferred_element_type=jnp.float32
    )
    grad_normed_part = jnp.einsum(
        "cef,edf->cd", grad_both, gate_up_low, preferred_element_type=jnp.float32
    )
    return (grad_gate_table, grad_normed_part, (sum_gate_up, sum_down))


def backward_rest(
    dense_set,
    saved,
    normed_ffn,
    selection,
    shares,
    grad_gate_table,
    grad_normed_part,
    grad_result,
    segment_row,
    cosine_table,
    sine_table,
    anchor,
):
    gains_low, query_low, keyvalue_low, out_low, router_low = dense_set
    (
        unit_first,
        inv_first,
        normed,
        grouped,
        shipped,
        attended,
        attended_low,
        log_totals,
        query_seg,
        query_pos,
        unit_second,
        inv_second,
    ) = saved
    kv_width = KV_HEADS * HEAD_DIM
    group_size = HEADS // KV_HEADS
    span_rows = grad_result.shape[0]
    grad_full = grad_result.astype(jnp.float32)
    grad_shares = jnp.sum(grad_gate_table[:, None, :] * selection, axis=-1)
    grad_chosen = shares * (grad_shares - jnp.sum(shares * grad_shares, axis=-1, keepdims=True))
    grad_logits = jnp.sum(grad_chosen[:, :, None] * selection, axis=1)
    grad_router = jnp.dot(normed_ffn.astype(jnp.float32).T, grad_logits, precision=HIGHEST)
    grad_normed_ffn = grad_normed_part + jnp.dot(
        grad_logits, router_low.astype(jnp.float32).T, precision=HIGHEST
    )
    gain_ffn = gains_low[1].astype(jnp.float32)
    gain_attn = gains_low[0].astype(jnp.float32)
    scaled_ffn = grad_normed_ffn * gain_ffn
    grad_gain_ffn = jnp.sum(grad_normed_ffn * unit_second, axis=0)
    grad_middle = grad_full + inv_second * (
        scaled_ffn - unit_second * jnp.mean(scaled_ffn * unit_second, axis=-1, keepdims=True)
    )
    grad_branch = grad_middle.astype(jnp.bfloat16)
    grad_out = jnp.einsum(
        "cd,ch->dh", grad_branch, attended_low, preferred_element_type=jnp.float32
    )
    grad_attended = jnp.dot(grad_branch, out_low, preferred_element_type=jnp.float32).astype(
        jnp.bfloat16
    )
    grad_grouped = grad_attended.reshape(span_rows, KV_HEADS, group_size, HEAD_DIM)
    products = (grad_attended.astype(jnp.float32) * attended).reshape(
        span_rows, KV_HEADS, group_size, HEAD_DIM
    )
    deltas = jnp.transpose(jnp.sum(products, axis=-1), (1, 2, 0))
    limit = anchor + span_rows
    start_state = (
        jnp.zeros((span_rows, KV_HEADS, group_size, HEAD_DIM), jnp.float32),
        jnp.zeros((segment_row.shape[0], 2 * kv_width), jnp.float32),
    )
    grad_query_rot, grad_keys_all = fold_backward(
        start_state,
        lax.all_gather(shipped, "ctx", axis=0, tiled=True),
        grouped,
        grad_grouped,
        log_totals,
        deltas,
        query_seg,
        query_pos,
        segment_row,
        limit,
    )
    grad_shipped = lax.psum_scatter(
        grad_keys_all.astype(jnp.bfloat16), "ctx", scatter_dimension=0, tiled=True
    ).astype(jnp.float32)
    grad_query_raw = (
        rotate(grad_query_rot.reshape(span_rows, HEADS, HEAD_DIM), cosine_table, -sine_table)
        .reshape(span_rows, HEADS * HEAD_DIM)
        .astype(jnp.bfloat16)
    )
    grad_key_raw = rotate(
        grad_shipped[:, :kv_width].reshape(span_rows, KV_HEADS, HEAD_DIM), cosine_table, -sine_table
    ).reshape(span_rows, kv_width)
    grad_keyvalue_raw = jnp.concatenate([grad_key_raw, grad_shipped[:, kv_width:]], axis=1).astype(
        jnp.bfloat16
    )
    grad_query = jnp.einsum("cd,ch->dh", normed, grad_query_raw, preferred_element_type=jnp.float32)
    grad_keyvalue = jnp.einsum(
        "cd,ch->dh", normed, grad_keyvalue_raw, preferred_element_type=jnp.float32
    )
    grad_normed = jnp.einsum(
        "ch,dh->cd", grad_query_raw, query_low, preferred_element_type=jnp.float32
    ) + jnp.einsum("ch,dh->cd", grad_keyvalue_raw, keyvalue_low, preferred_element_type=jnp.float32)
    scaled_attn = grad_normed * gain_attn
    grad_gain_attn = jnp.sum(grad_normed * unit_first, axis=0)
    input_grad = grad_middle + inv_first * (
        scaled_attn - unit_first * jnp.mean(scaled_attn * unit_first, axis=-1, keepdims=True)
    )
    grad_gains = jnp.stack([grad_gain_attn, grad_gain_ffn])
    return ((grad_gains, grad_query, grad_keyvalue, grad_out, grad_router), input_grad)


def adamw_step(weight, gradient, moment, second, step_rate, decay_rate):
    moment_new = BETA_ONE * moment + (1.0 - BETA_ONE) * gradient
    second_new = BETA_TWO * second + (1.0 - BETA_TWO) * gradient * gradient
    moment_hat = moment_new / (1.0 - BETA_ONE**STEP)
    second_hat = second_new / (1.0 - BETA_TWO**STEP)
    weight_new = weight - step_rate * (
        moment_hat / (jnp.sqrt(second_hat) + EPS_ADAM) + decay_rate * weight
    )
    return (moment_new, second_new, weight_new)


def body(
    inputs,
    cotangent,
    routes,
    segments,
    gains,
    gains_first,
    gains_second,
    w_query,
    query_first,
    query_second,
    w_keyvalue,
    keyvalue_first,
    keyvalue_second,
    w_out,
    out_first,
    out_second,
    w_router,
    router_first,
    router_second,
    w_gate_up,
    gate_up_first,
    gate_up_second,
    w_down,
    down_first,
    down_second,
):
    span_rows = inputs.shape[2]
    micro_count = inputs.shape[0]
    anchor = lax.axis_index("ctx") * span_rows
    cosine_table, sine_table = rope_tables(anchor + jnp.arange(span_rows, dtype=jnp.int32))
    weights = (gains, w_query, w_keyvalue, w_out, w_router, w_gate_up, w_down)
    firsts = (
        gains_first,
        query_first,
        keyvalue_first,
        out_first,
        router_first,
        gate_up_first,
        down_first,
    )
    seconds = (
        gains_second,
        query_second,
        keyvalue_second,
        out_second,
        router_second,
        gate_up_second,
        down_second,
    )
    gate_up_low = w_gate_up.astype(jnp.bfloat16)
    down_low = w_down.astype(jnp.bfloat16)
    dense_set = (
        lax.all_gather(gains.astype(jnp.bfloat16), ("batch", "ctx"), axis=1, tiled=True),
        lax.all_gather(w_query.astype(jnp.bfloat16), ("batch", "ctx"), axis=0, tiled=True),
        lax.all_gather(w_keyvalue.astype(jnp.bfloat16), ("batch", "ctx"), axis=0, tiled=True),
        lax.all_gather(w_out.astype(jnp.bfloat16), ("batch", "ctx"), axis=0, tiled=True),
        lax.all_gather(w_router.astype(jnp.bfloat16), ("batch", "ctx"), axis=0, tiled=True),
    )
    expert_set = (
        lax.all_gather(gate_up_low, ("batch", "ctx"), axis=1, tiled=True),
        lax.all_gather(down_low, ("batch", "ctx"), axis=1, tiled=True),
    )
    expert_sums = (
        jnp.zeros(expert_set[0].shape, jnp.float32),
        jnp.zeros(expert_set[1].shape, jnp.float32),
    )
    dense_sums = None
    result_list = []
    input_list = []
    for micro_index in range(micro_count):
        tokens = inputs[micro_index, 0].astype(jnp.float32)
        cot_span = cotangent[micro_index, 0]
        segment_row = segments[micro_index, 0]
        route_row = routes[micro_index, 0]
        middle, normed_ffn, saved = attention_forward(
            dense_set, tokens, segment_row, cosine_table, sine_table, anchor
        )
        route_span = lax.dynamic_slice_in_dim(route_row, anchor, span_rows, 0)
        selection, shares, gate_table = route_gates(normed_ffn, dense_set[4], route_span)
        expert_sum, kept_rows = experts_forward(
            normed_ffn, gate_table, expert_set[0], expert_set[1]
        )
        result_list.append((middle + expert_sum).astype(jnp.bfloat16))
        grad_gate_table, grad_normed_part, expert_sums = experts_backward(
            cot_span, normed_ffn, gate_table, kept_rows, expert_set[0], expert_set[1], expert_sums
        )
        micro_grads, input_grad = backward_rest(
            dense_set,
            saved,
            normed_ffn,
            selection,
            shares,
            grad_gate_table,
            grad_normed_part,
            cot_span,
            segment_row,
            cosine_table,
            sine_table,
            anchor,
        )
        input_list.append(input_grad)
        dense_sums = (
            micro_grads
            if dense_sums is None
            else tuple((left + right for left, right in zip(dense_sums, micro_grads)))
        )
    owned_dense = (
        lax.psum_scatter(dense_sums[0], ("batch", "ctx"), scatter_dimension=1, tiled=True),
        lax.psum_scatter(dense_sums[1], ("batch", "ctx"), scatter_dimension=0, tiled=True),
        lax.psum_scatter(dense_sums[2], ("batch", "ctx"), scatter_dimension=0, tiled=True),
        lax.psum_scatter(dense_sums[3], ("batch", "ctx"), scatter_dimension=0, tiled=True),
        lax.psum_scatter(dense_sums[4], ("batch", "ctx"), scatter_dimension=0, tiled=True),
    )
    grad_gate_up_owned, grad_down_owned = (
        lax.psum_scatter(expert_sums[0], ("batch", "ctx"), scatter_dimension=1, tiled=True),
        lax.psum_scatter(expert_sums[1], ("batch", "ctx"), scatter_dimension=1, tiled=True),
    )
    owned_grads = tuple(owned_dense) + (grad_gate_up_owned, grad_down_owned)
    updated = []
    for kind_index in range(7):
        updated.extend(
            adamw_step(
                weights[kind_index],
                owned_grads[kind_index],
                firsts[kind_index],
                seconds[kind_index],
                RATES[kind_index],
                DECAYS[kind_index],
            )
        )
    outputs = jnp.stack(result_list)[:, None]
    input_grads = jnp.stack(input_list)[:, None]
    (
        gains_moment,
        gains_square,
        gains_new,
        query_moment,
        query_square,
        query_new,
        keyvalue_moment,
        keyvalue_square,
        keyvalue_new,
        out_moment,
        out_square,
        out_new,
        router_moment,
        router_square,
        router_new,
        gate_up_moment,
        gate_up_square,
        gate_up_new,
        down_moment,
        down_square,
        down_new,
    ) = updated
    return (
        outputs,
        input_grads,
        gains_moment,
        gains_square,
        gains_new,
        query_moment,
        query_square,
        query_new,
        keyvalue_moment,
        keyvalue_square,
        keyvalue_new,
        out_moment,
        out_square,
        out_new,
        router_moment,
        router_square,
        router_new,
        gate_up_moment,
        gate_up_square,
        gate_up_new,
        down_moment,
        down_square,
        down_new,
    )


def solution(mesh):
    placed = (
        P(None, "batch", "ctx", None),
        P(None, "batch", "ctx", None),
        P(None, "batch", None, None),
        P(None, "batch", None),
        P(None, ("batch", "ctx")),
        P(None, ("batch", "ctx")),
        P(None, ("batch", "ctx")),
        P(("batch", "ctx"), None),
        P(("batch", "ctx"), None),
        P(("batch", "ctx"), None),
        P(("batch", "ctx"), None),
        P(("batch", "ctx"), None),
        P(("batch", "ctx"), None),
        P(("batch", "ctx"), None),
        P(("batch", "ctx"), None),
        P(("batch", "ctx"), None),
        P(("batch", "ctx"), None),
        P(("batch", "ctx"), None),
        P(("batch", "ctx"), None),
        P(None, ("batch", "ctx"), None),
        P(None, ("batch", "ctx"), None),
        P(None, ("batch", "ctx"), None),
        P(None, ("batch", "ctx"), None),
        P(None, ("batch", "ctx"), None),
        P(None, ("batch", "ctx"), None),
    )
    return jax.shard_map(
        body,
        mesh=mesh,
        in_specs=placed,
        out_specs=(
            P(None, "batch", "ctx", None),
            P(None, "batch", "ctx", None),
            P(None, ("batch", "ctx")),
            P(None, ("batch", "ctx")),
            P(None, ("batch", "ctx")),
            P(("batch", "ctx"), None),
            P(("batch", "ctx"), None),
            P(("batch", "ctx"), None),
            P(("batch", "ctx"), None),
            P(("batch", "ctx"), None),
            P(("batch", "ctx"), None),
            P(("batch", "ctx"), None),
            P(("batch", "ctx"), None),
            P(("batch", "ctx"), None),
            P(("batch", "ctx"), None),
            P(("batch", "ctx"), None),
            P(("batch", "ctx"), None),
            P(None, ("batch", "ctx"), None),
            P(None, ("batch", "ctx"), None),
            P(None, ("batch", "ctx"), None),
            P(None, ("batch", "ctx"), None),
            P(None, ("batch", "ctx"), None),
            P(None, ("batch", "ctx"), None),
        ),
        check_vma=False,
    )
```

profile of v0, /device:TPU:10, one launch (start us, length us, event | category | flops | bytes accessed | tf_op | source)
XLA Modules:
  0.0 3950.3 jit_solution(1558437466667499219)
XLA Ops:
  11.2 58.9 %all-gather = bf16[32,32,2]{1,2,0:T(2,128)(2,1)S(1)} all-gather(bf16[1,32,2]{1,2,0:T(2,128)(2,1)S(1)} %convert_bitcast_fusion.3), channel_id=1, replica_groups=mesh['batch'=2,'ctx'=16] {'batch','ctx'}, dimensions={0}, use_global_device_ids=true | all-gather | bytes 4224 | tf_op jit(solution)/shard_map/all_gather | solution.py:450
  87.0 69.6 %all-gather.1 = bf16[32,32,16]{1,2,0:T(8,128)(2,1)S(1)} all-gather(bf16[1,32,16]{1,2,0:T(8,128)(2,1)S(1)} %convert_bitcast_fusion.2), channel_id=1, replica_groups=mesh['batch'=2,'ctx'=16] {'batch','ctx'}, dimensions={0}, use_global_device_ids=true | all-gather | bytes 33792 | tf_op jit(solution)/shard_map/all_gather | solution.py:454
  158.2 2.9 copy.165
  163.0 35.6 all-gather.12.cloned.1.call-done
  198.6 4.7 copy.166
  203.3 65.2 %all-gather.22.cloned.1.call-done = bf16[1536,1024]{1,0:T(8,128)(2,1)} async-done(((bf16[96,1024]{1,0:T(8,128)(2,1)}), bf16[1536,1024]{1,0:T(8,128)(2,1)}) %all-gather.22.cloned.1.call-update) | async-done | bytes 3145744 | tf_op jit(solution)/shard_map/all_gather | solution.py:195
  268.5 4.6 copy.170
  273.2 18.1 while.56
  274.5 7.1 conditional.12
  282.9 7.1 conditional.12
  292.4 18.6 while.57
  293.6 7.1 conditional.13
  302.0 7.1 conditional.13
  311.8 14.0 all-gather.16.cloned.1.call-done
  330.5 190.7 %all-gather.18.cloned.1.call-done = bf16[16,1024,1024]{2,1,0:T(8,128)(2,1)} async-done(((bf16[16,32,1024]{2,1,0:T(8,128)(2,1)}), bf16[16,1024,1024]{2,1,0:T(8,128)(2,1)}) %all-gather.18.cloned.1.call-update) | async-done | bytes 33554448 | tf_op jit(solution)/shard_map/all_gather | solution.py:457
  521.2 18.5 fusion.133
  539.7 99.5 %all-gather.20.cloned.1.call-done = bf16[16,1024,512]{2,1,0:T(8,128)(2,1)} async-done(((bf16[16,32,512]{2,1,0:T(8,128)(2,1)}), bf16[16,1024,512]{2,1,0:T(8,128)(2,1)}) %all-gather.20.cloned.1.call-update) | async-done | bytes 16777232 | tf_op jit(solution)/shard_map/all_gather | solution.py:458
  639.2 13.4 multiply_reduce_fusion.1
  652.8 5.6 multiply_convert_fusion.3
  658.5 17.9 fusion.75
  676.3 2.8 multiply_reduce_fusion.3
  679.3 18.6 fusion.129
  697.9 13.5 multiply_reduce_fusion
  711.5 5.6 multiply_convert_fusion.1
  717.2 17.9 fusion.76
  741.1 3.4 broadcast.608.clone
  744.6 50.1 %while.58 = (s32[]{:T(128)}, f32[96,8,2,64]{0,3,2,1:T(8,128)S(1)}, f32[1536,1024]{0,1:T(8,128)}, s32[3]{0:T(128)S(1)}, s32[]{:T(128)}, /*index=5*/s32[96]{0:T(12...) while((s32[]{:T(128)}, f32[96,8,2,64]{0,3,2,1:T(8,128)S(1)}, ...), condition=%wide.region_33.34_spmd.clone, body=%wide.region_30.0_spmd.clone.sunk | while | flops 514409056 | bytes 34257136 | solution.py:160
  745.8 23.2 conditional.14
  758.4 10.5 dynamic_update_slice.6
  770.2 23.1 conditional.14
  782.8 10.5 dynamic_update_slice.6
  794.7 4.8 convert_element_type.256
  799.5 4.6 copy.209
  811.6 3.4 broadcast.608.clone.1
  815.0 50.5 %while.59 = (s32[]{:T(128)}, f32[96,8,2,64]{0,3,2,1:T(8,128)S(1)}, f32[1536,1024]{0,1:T(8,128)}, s32[3]{0:T(128)S(1)}, s32[]{:T(128)}, /*index=5*/s32[96]{0:T(12...) while((s32[]{:T(128)}, f32[96,8,2,64]{0,3,2,1:T(8,128)S(1)}, ...), condition=%wide.region_45.46_spmd.clone, body=%wide.region_42.45_spmd.clone.sunk | while | flops 514409056 | bytes 34257136 | solution.py:160
  816.7 23.2 conditional.15
  829.3 10.6 dynamic_update_slice.7
  841.1 23.2 conditional.15
  853.7 10.5 dynamic_update_slice.7
  865.6 4.9 convert_element_type.263
  870.5 4.7 copy.211
  877.9 4.2 fusion.147
  885.3 71.3 %reduce-scatter.28.cloned.1.call-done = bf16[96,1024]{1,0:T(8,128)(2,1)} async-done(((bf16[1536,1024]{1,0:T(8,128)(2,1)}), bf16[96,1024]{1,0:T(8,128)(2,1)}) %reduce-scatter.28.cloned.1.call-update) | async-done | bytes 196624
  958.5 133.0 %reduce-scatter.30.cloned.1.call-done = bf16[96,1024]{1,0:T(8,128)(2,1)} async-done(((bf16[1536,1024]{1,0:T(8,128)(2,1)}), bf16[96,1024]{1,0:T(8,128)(2,1)}) %reduce-scatter.30.cloned.1.call-update) | async-done | bytes 196624
  1095.2 3.4 fusion.104
  1099.8 5.0 convolution_add_fusion
  1106.6 2.9 convolution_add_fusion.2
  1111.3 2.8 convolution_add_fusion.1
  1116.1 13.4 fusion.85
  1129.5 21.4 add_bitcast_fusion.1
  1150.9 34.2 copy.185
  1186.1 25.3 fusion.73
  1211.4 42.7 %add_bitcast_fusion = f32[16,1024,1024]{1,2,0:T(8,128)} fusion(f32[16,1024,1024]{2,1,0:T(8,128)} %fusion.73, bf16[96,16,512]{2,0,1:T(8,128)(2,1)S(1)} %copy-done.13, bf16[96,16,512]{2,0,1:T(8,128)(2,1)S(1)} %copy-done.12, bf16[96,1024]{1,0:T(8,128)(2,1)S(1)} %copy-done.30), kind=kOutput, calls=%fused_computation.88 | convolution fusion | flops 3244294144 | bytes 137560064 | tf_op jit(solution)/shard_map/cd,cef->edf/dot_general | solution.py:271
  1254.1 65.8 %copy.180 = f32[16,1024,1024]{2,0,1:T(8,128)} copy(f32[16,1024,1024]{1,2,0:T(8,128)} %add_bitcast_fusion) | data formatting | bytes 134217728 | tf_op jit(solution)/shard_map/add | solution.py:271
  1321.8 11.8 fusion.81
  1333.8 12.1 fusion.82
  1349.5 8.6 reduce-scatter.32.cloned.1.call-done
  1359.4 145.3 %reduce-scatter.22.cloned.1.call-done = f32[32,1024]{1,0:T(8,128)} async-done(((f32[1024,1024]{1,0:T(8,128)}), f32[32,1024]{1,0:T(8,128)}) %reduce-scatter.22.cloned.1.call-update) | async-done | bytes 131088 | tf_op jit(solution)/shard_map/reduce_scatter | solution.py:508
  1506.6 145.5 %reduce-scatter.18.cloned.1.call-done = f32[32,1024]{1,0:T(8,128)} async-done(((f32[1024,1024]{1,0:T(8,128)}), f32[32,1024]{1,0:T(8,128)}) %reduce-scatter.18.cloned.1.call-update) | async-done | bytes 131088 | tf_op jit(solution)/shard_map/reduce_scatter | solution.py:506
  1653.9 144.4 %reduce-scatter.20.cloned.1.call-done = f32[32,1024]{1,0:T(8,128)} async-done(((f32[1024,1024]{1,0:T(8,128)}), f32[32,1024]{1,0:T(8,128)}) %reduce-scatter.20.cloned.1.call-update) | async-done | bytes 131088 | tf_op jit(solution)/shard_map/reduce_scatter | solution.py:507
  1800.3 717.2 %reduce-scatter.26.cloned.1.call-done = f32[16,32,512]{2,0,1:T(8,128)} async-done(((f32[16,1024,512]{2,0,1:T(8,128)}), f32[16,32,512]{2,0,1:T(8,128)}) %reduce-scatter.26.cloned.1.call-update) | async-done | bytes 1048592 | tf_op jit(solution)/shard_map/reduce_scatter | solution.py:513
  2517.5 3.6 multiply_subtract_fusion.1
  2525.8 1402.1 %reduce-scatter.24.cloned.1.call-done = f32[16,32,1024]{2,0,1:T(8,128)} async-done(((f32[16,1024,1024]{2,0,1:T(8,128)}), f32[16,32,1024]{2,0,1:T(8,128)}) %reduce-scatter.24.cloned.1.call-update) | async-done | bytes 2097168 | tf_op jit(solution)/shard_map/reduce_scatter | solution.py:512
  3927.9 7.8 multiply_subtract_fusion
  (483 shorter events, 157.8 us)
Async XLA Ops:
  7.2 68.8 %copy-start.6 = (bf16[2,1,96,1024]{3,2,1,0:T(8,128)(2,1)S(1)}, bf16[2,1,96,1024]{3,2,1,0:T(8,128)(2,1)}, u32[]{:S(2)}) copy-start(bf16[2,1,96,1024]{3,2,1,0:T(8,128)(2,1)} %param.41) | copy-start | bytes 1179652
  7.2 65.1 %all-gather.10.cloned.1.call-start = ((), (), s32[]{:S(2)}) async-start(), calls=%async_computation.9 | async-start | bytes 2162688 | tf_op jit(solution)/shard_map/all_gather | solution.py:452
  8.9 149.4 %all-gather.14.cloned.1.call-start = ((), (), s32[]{:S(2)}) async-start(), calls=%async_computation.11 | async-start | bytes 2162688 | tf_op jit(solution)/shard_map/all_gather | solution.py:451
  10.5 188.1 %all-gather.12.cloned.1.call-start = ((), (), s32[]{:S(2)}) async-start(), calls=%async_computation.10 | async-start | bytes 3342336 | tf_op jit(solution)/shard_map/all_gather | solution.py:195
  71.5 90.4 %copy-start.57 = (f32[1,1024]{1,0:T(1,128)}, f32[1,1024]{1,0:T(1,128)S(1)}, u32[]{:S(2)}) copy-start(f32[1,1024]{1,0:T(1,128)S(1)} %get-tuple-element.1168) | copy-start | bytes 12292
  81.0 187.5 %all-gather.22.cloned.1.call-start = ((), (), s32[]{:S(2)}) async-start(), calls=%async_computation.15 | async-start | bytes 3342336 | tf_op jit(solution)/shard_map/all_gather | solution.py:195
  82.8 243.0 %all-gather.16.cloned.1.call-start = ((), (), s32[]{:S(2)}) async-start(), calls=%async_computation.12 | async-start | bytes 2162688 | tf_op jit(solution)/shard_map/all_gather | solution.py:453
  83.5 73.8 %copy-start.88 = (s32[2,1,1536]{2,1,0:T(1,128)S(1)}, s32[2,1,1536]{2,1,0:T(1,128)}, u32[]{:S(2)}) copy-start(s32[2,1,1536]{2,1,0:T(1,128)} %param.44) | copy-start | bytes 36868
  83.5 74.0 %copy-start.71 = (s32[2,1,1536,8]{2,3,1,0:T(8,128)S(1)}, s32[2,1,1536,8]{2,3,1,0:T(8,128)}, u32[]{:S(2)}) copy-start(s32[2,1,1536,8]{2,3,1,0:T(8,128)} %param.43) | copy-start | bytes 294916
  83.5 437.7 %all-gather.18.cloned.1.call-start = ((), (), s32[]{:S(2)}) async-start(), calls=%async_computation.13 | async-start | bytes 34603008 | tf_op jit(solution)/shard_map/all_gather | solution.py:457
  84.8 554.4 %all-gather.20.cloned.1.call-start = ((), (), s32[]{:S(2)}) async-start(), calls=%async_computation.14 | async-start | bytes 17301504 | tf_op jit(solution)/shard_map/all_gather | solution.py:458
  86.9 74.2 %copy-start.79 = (f32[96]{0:T(128)S(1)}, f32[96]{0:T(128)}, u32[]{:S(2)}) copy-start(f32[96]{0:T(128)} %copy-done.78) | copy-start | bytes 1156
  86.9 869.6 %reduce-scatter.28.cloned.1.call-start = ((), (), s32[]{:S(2)}) async-start(), calls=%async_computation.21 | async-start | bytes 3342336
  328.6 408.6 %copy-start.14 = (f32[96,1024]{1,0:T(8,128)}, f32[96,1024]{1,0:T(8,128)S(1)}, u32[]{:S(2)}) copy-start(f32[96,1024]{1,0:T(8,128)S(1)} %get-tuple-element.1176) | copy-start | bytes 1179652
  330.3 209.4 %copy-start.31 = (bf16[96,1024]{1,0:T(8,128)(2,1)}, bf16[96,1024]{1,0:T(8,128)(2,1)S(1)}, u32[]{:S(2)}) copy-start(bf16[96,1024]{1,0:T(8,128)(2,1)S(1)} %multiply_convert_fusion.11) | copy-start | bytes 589828
  539.7 112.9 %copy-start.75 = (s32[96,8]{0,1:T(8,128)S(1)}, s32[96,8]{0,1:T(8,128)}, u32[]{:S(2)}) copy-start(s32[96,8]{0,1:T(8,128)} %get-tuple-element.1186) | copy-start | bytes 9220
  652.8 23.5 copy-start.72
  658.5 17.9 copy-start.17
  679.1 18.8 copy-start.28
  679.3 18.6 copy-start.43
  697.9 13.5 copy-start.74
  804.1 287.4 %reduce-scatter.30.cloned.1.call-start = ((), (), s32[]{:S(2)}) async-start(), calls=%async_computation.22 | async-start | bytes 3342336
  875.3 471.5 %reduce-scatter.34.cloned.1.call-start = ((), (), s32[]{:S(2)}) async-start(), calls=%async_computation.24 | async-start | bytes 540672
  882.1 475.9 %reduce-scatter.32.cloned.1.call-start = ((), (), s32[]{:S(2)}) async-start(), calls=%async_computation.23 | async-start | bytes 540672
  883.0 209.8 %copy-start.62 = (f32[96,32]{0,1:T(8,128)S(1)}, f32[96,32]{0,1:T(8,128)}, u32[]{:S(2)}) copy-start(f32[96,32]{0,1:T(8,128)} %get-tuple-element.1171) | copy-start | bytes 36868
  883.7 210.6 %copy-start.1 = (bf16[1024,1024]{1,0:T(8,128)(2,1)S(1)}, bf16[1024,1024]{1,0:T(8,128)(2,1)}, u32[]{:S(2)}) copy-start(bf16[1024,1024]{1,0:T(8,128)(2,1)} %all-gather.10.cloned.1.call-done) | copy-start | bytes 6291460
  957.6 137.5 %copy-start.7 = (bf16[2,1,96,1024]{3,2,1,0:T(8,128)(2,1)S(1)}, bf16[2,1,96,1024]{3,2,1,0:T(8,128)(2,1)}, u32[]{:S(2)}) copy-start(bf16[2,1,96,1024]{3,2,1,0:T(8,128)(2,1)} %param.41) | copy-start | bytes 1179652
  957.6 137.5 %copy-start.58 = (f32[1,1024]{1,0:T(1,128)S(1)}, f32[1,1024]{1,0:T(1,128)}, u32[]{:S(2)}) copy-start(f32[1,1024]{1,0:T(1,128)} %copy-done.57) | copy-start | bytes 12292
  957.7 137.5 %copy-start.80 = (f32[96]{0:T(128)S(1)}, f32[96]{0:T(128)}, u32[]{:S(2)}) copy-start(f32[96]{0:T(128)} %copy-done.78) | copy-start | bytes 1156
  957.7 137.5 %copy-start.84 = (f32[96]{0:T(128)S(1)}, f32[96]{0:T(128)}, u32[]{:S(2)}) copy-start(f32[96]{0:T(128)} %copy-done.82) | copy-start | bytes 1156
  1099.7 405.0 %reduce-scatter.22.cloned.1.call-start = ((), (), s32[]{:S(2)}) async-start(), calls=%async_computation.18 | async-start | bytes 4325376 | tf_op jit(solution)/shard_map/reduce_scatter | solution.py:508
  1104.8 547.3 %reduce-scatter.18.cloned.1.call-start = ((), (), s32[]{:S(2)}) async-start(), calls=%async_computation.16 | async-start | bytes 4325376 | tf_op jit(solution)/shard_map/reduce_scatter | solution.py:506
  1109.5 688.8 %reduce-scatter.20.cloned.1.call-start = ((), (), s32[]{:S(2)}) async-start(), calls=%async_computation.17 | async-start | bytes 4325376 | tf_op jit(solution)/shard_map/reduce_scatter | solution.py:507
  1114.2 1403.3 %reduce-scatter.26.cloned.1.call-start = ((), (), s32[]{:S(2)}) async-start(), calls=%async_computation.20 | async-start | bytes 34603008 | tf_op jit(solution)/shard_map/reduce_scatter | solution.py:513
  1116.1 13.4 copy-start.9
  1116.1 13.4 copy-start.64
  1185.2 26.2 copy-start.12
  1185.2 26.2 copy-start.13
  1185.2 26.2 copy-start.30
  1185.2 2742.6 %reduce-scatter.24.cloned.1.call-start = ((), (), s32[]{:S(2)}) async-start(), calls=%async_computation.19 | async-start | bytes 69206016 | tf_op jit(solution)/shard_map/reduce_scatter | solution.py:512
  1321.8 11.8 copy-start.65
  1333.6 12.3 copy-start.53
  1333.6 13.9 copy-start.77
  1333.6 13.9 copy-start.89
  1333.6 13.9 copy-start.90
  1333.6 14.5 copy-start.95
  1333.7 14.5 copy-start.94
  1333.7 14.5 copy-start.8
  1333.7 14.5 copy-start.25
  1333.7 14.5 copy-start.27
  1333.7 14.5 copy-start.36
  1333.7 14.5 copy-start.42
  1333.7 14.5 copy-start.59
  1333.7 14.5 copy-start.81
  1333.7 14.5 copy-start.85
  1345.9 12.9 copy-start.91
  1345.9 12.9 copy-start.92
  1345.9 12.9 copy-start.93
  1345.9 158.8 %copy-start.55 = (f32[32,1024]{1,0:T(8,128)S(1)}, f32[32,1024]{1,0:T(8,128)}, u32[]{:S(2)}) copy-start(f32[32,1024]{1,0:T(8,128)} %param.54) | copy-start | bytes 393220
  1345.9 306.2 %copy-start.56 = (f32[32,1024]{1,0:T(8,128)S(1)}, f32[32,1024]{1,0:T(8,128)}, u32[]{:S(2)}) copy-start(f32[32,1024]{1,0:T(8,128)} %param.48) | copy-start | bytes 393220
  1348.2 1169.2 %copy-start.34 = (f32[16,32,512]{2,1,0:T(8,128)S(1)}, f32[16,32,512]{2,1,0:T(8,128)}, u32[]{:S(2)}) copy-start(f32[16,32,512]{2,1,0:T(8,128)} %param.63) | copy-start | bytes 3145732
  1348.5 1169.0 %copy-start.51 = (f32[16,32,512]{2,1,0:T(8,128)S(1)}, f32[16,32,512]{2,1,0:T(8,128)}, u32[]{:S(2)}) copy-start(f32[16,32,512]{2,1,0:T(8,128)} %param.65) | copy-start | bytes 3145732
  1348.5 1169.0 %copy-start.52 = (f32[16,32,512]{2,1,0:T(8,128)S(1)}, f32[16,32,512]{2,1,0:T(8,128)}, u32[]{:S(2)}) copy-start(f32[16,32,512]{2,1,0:T(8,128)} %param.64) | copy-start | bytes 3145732
  2521.0 1406.9 %copy-start.19 = (f32[16,32,1024]{2,1,0:T(8,128)S(1)}, f32[16,32,1024]{2,1,0:T(8,128)}, u32[]{:S(2)}) copy-start(f32[16,32,1024]{2,1,0:T(8,128)} %param.60) | copy-start | bytes 6291460
  (49 other events, 152.1 us)
Sparse Core Ops, SparseCore 0:
  11.5 56.5 all-gather.9
  71.5 55.3 all-gather.13
  130.3 68.2 all-gather.11
  201.8 66.6 all-gather.21
  271.8 53.9 all-gather.15
  329.1 192.0 all-gather.17
  524.7 114.4 all-gather.19
  804.3 152.2 reduce-scatter.27
  961.5 129.9 reduce-scatter.29
  1094.2 126.8 reduce-scatter.33
  1224.0 133.9 reduce-scatter.31
  1360.2 144.5 reduce-scatter.21
  1507.0 145.0 reduce-scatter.17
  1654.2 144.0 reduce-scatter.19
  1800.5 716.9 reduce-scatter.25
  2519.7 1408.1 reduce-scatter.23
where the time goes:
time: 3960 us; the launch traced here: 3950 us
  waiting for transfers between devices  3170 us (80%)
  matrix products  297 us (8%)
  local copies, waits for them, and re-layouts  229 us (6%)
  blocking collectives  129 us (3%)
  other arithmetic  81 us (2%)
    reduce_scatter x1, waiting for transfers between devices, body(): lax.psum_scatter(expert_sums[0], ('batch', 'ctx'), scatter_dimension=1, t...  1400 us
    reduce_scatter x1, waiting for transfers between devices, body(): lax.psum_scatter(expert_sums[1], ('batch', 'ctx'), scatter_dimension=1, t...  717 us
    unnamed x20, waiting for transfers between devices  213 us
    all_gather x1, waiting for transfers between devices, body(): lax.all_gather(gate_up_low, ('batch', 'ctx'), axis=1, tiled=True)  191 us
    reduce_scatter x1, waiting for transfers between devices, body(): lax.psum_scatter(dense_sums[1], ('batch', 'ctx'), scatter_dimension=0, ti...  146 us
    reduce_scatter x1, waiting for transfers between devices, body(): lax.psum_scatter(dense_sums[3], ('batch', 'ctx'), scatter_dimension=0, ti...  145 us
    reduce_scatter x1, waiting for transfers between devices, body(): lax.psum_scatter(dense_sums[2], ('batch', 'ctx'), scatter_dimension=0, ti...  144 us
    all_gather x2, waiting for transfers between devices, attention_forward(): lax.all_gather(shipped, 'ctx', axis=0, tiled=True)  101 us
  transfers between devices with their start and end apart: 16, of which 13 were waited for; matrix products, arithmetic and copies ran while one was open for 11% of the time, Pallas kernels for 0%

commit v1 on v0

v1 whole, which is shorter than its diff:
```python
import math

import jax
import jax.numpy as jnp
from jax import lax
from jax.sharding import PartitionSpec as P

HEADS = 16
KV_HEADS = 8
HEAD_DIM = 64
FF = 512
EXPERTS = 16
STEP = 10


EPS_NORM = 1e-06
EPS_ADAM = 1e-08
BETA_ONE = 0.9
BETA_TWO = 0.95
MASKED = -1e30
ROPE_BASE = 10000.0
RATES = (1.0, 0.04, 0.1, 1.5, 0.02, 0.1, 0.2)
DECAYS = (0.0, 0.1, 0.1, 0.1, 0.1, 0.1, 0.1)
HIGHEST = lax.Precision.HIGHEST


def rope_tables(positions):
    half_width = HEAD_DIM // 2
    frequency = ROPE_BASE ** (-(jnp.arange(half_width, dtype=jnp.float32) * 2.0) / HEAD_DIM)
    angles = positions.astype(jnp.float32)[:, None] * frequency[None, :]
    return (jnp.cos(angles), jnp.sin(angles))


def rotate(values, cosine_table, sine_table):
    half_width = values.shape[-1] // 2
    first_half = values[..., :half_width]
    second_half = values[..., half_width:]
    cos_rows = cosine_table[:, None, :]
    sin_rows = sine_table[:, None, :]
    return jnp.concatenate(
        [
            first_half * cos_rows - second_half * sin_rows,
            second_half * cos_rows + first_half * sin_rows,
        ],
        axis=-1,
    )


def prepare_blocks(shard_rows):
    total_rows = shard_rows.shape[0]
    step_rows = math.gcd(total_rows, 512)
    blocks = shard_rows.reshape(total_rows // step_rows, step_rows, shard_rows.shape[1])
    offsets = jnp.arange(total_rows // step_rows, dtype=jnp.int32) * step_rows
    return (blocks, offsets, step_rows)


def block_scores(grouped, block_rows, key_start, step_rows, query_seg, query_pos, segment_row):
    kv_width = KV_HEADS * HEAD_DIM
    key_rows = block_rows[:, :kv_width].reshape(step_rows, KV_HEADS, HEAD_DIM)
    value_rows = block_rows[:, kv_width:].reshape(step_rows, KV_HEADS, HEAD_DIM)
    key_seg = lax.dynamic_slice_in_dim(segment_row, key_start, step_rows)
    key_pos = key_start + jnp.arange(step_rows, dtype=jnp.int32)
    allowed = ((query_seg[:, None] == key_seg[None, :]) & (query_pos[:, None] >= key_pos[None, :]))[
        None, None
    ]
    scores = jnp.einsum(
        "cgrd,kgd->grck", grouped, key_rows, preferred_element_type=jnp.float32
    ) * HEAD_DIM ** (-0.5)
    return (key_rows, value_rows, allowed, jnp.where(allowed, scores, MASKED))


def fold_forward(running, shard_rows, grouped, query_seg, query_pos, segment_row, limit):
    blocks, offsets, step_rows = prepare_blocks(shard_rows)

    def visit(current, block_pair):
        block_rows, offset = block_pair

        def attend(inner):
            maxima, totals, accumulated = inner
            key_rows, value_rows, allowed, scores = block_scores(
                grouped, block_rows, offset, step_rows, query_seg, query_pos, segment_row
            )
            new_max = jnp.maximum(maxima, jnp.max(scores, axis=-1))
            fading = jnp.exp(maxima - new_max)
            block_weights = jnp.where(allowed, jnp.exp(scores - new_max[..., None]), 0.0)
            totals = totals * fading + jnp.sum(block_weights, axis=-1)
            update = jnp.einsum(
                "grck,kgd->cgrd",
                block_weights.astype(jnp.bfloat16),
                value_rows,
                preferred_element_type=jnp.float32,
            )
            accumulated = accumulated * jnp.transpose(fading, (2, 0, 1))[..., None] + update
            return (new_max, totals, accumulated)

        return (lax.cond(offset < limit, attend, lambda inner: inner, current), None)

    running, unused = lax.scan(visit, running, (blocks, offsets))
    return running


def fold_backward(
    running,
    shard_rows,
    grouped,
    grad_grouped,
    log_totals,
    deltas,
    query_seg,
    query_pos,
    segment_row,
    limit,
):
    blocks, offsets, step_rows = prepare_blocks(shard_rows)
    kv_width = KV_HEADS * HEAD_DIM
    factor = HEAD_DIM ** (-0.5)

    def visit(current, block_pair):
        block_rows, offset = block_pair

        def attend(inner):
            grad_query, grad_keys = inner
            key_rows, value_rows, allowed, scores = block_scores(
                grouped, block_rows, offset, step_rows, query_seg, query_pos, segment_row
            )
            block_weights = jnp.where(allowed, jnp.exp(scores - log_totals[..., None]), 0.0)
            grad_weights = jnp.einsum(
                "cgrd,kgd->grck", grad_grouped, value_rows, preferred_element_type=jnp.float32
            )
            grad_scores = (block_weights * (grad_weights - deltas[..., None])).astype(jnp.bfloat16)
            grad_query = (
                grad_query
                + jnp.einsum(
                    "grck,kgd->cgrd", grad_scores, key_rows, preferred_element_type=jnp.float32
                )
                * factor
            )
            key_part = (
                jnp.einsum(
                    "grck,cgrd->kgd", grad_scores, grouped, preferred_element_type=jnp.float32
                )
                * factor
            )
            value_part = jnp.einsum(
                "grck,cgrd->kgd",
                block_weights.astype(jnp.bfloat16),
                grad_grouped,
                preferred_element_type=jnp.float32,
            )
            block_grad = jnp.concatenate(
                [key_part.reshape(step_rows, kv_width), value_part.reshape(step_rows, kv_width)],
                axis=1,
            )
            previous = lax.dynamic_slice_in_dim(grad_keys, offset, step_rows, 0)
            grad_keys = lax.dynamic_update_slice_in_dim(grad_keys, previous + block_grad, offset, 0)
            return (grad_query, grad_keys)

        return (lax.cond(offset < limit, attend, lambda inner: inner, current), None)

    running, unused = lax.scan(visit, running, (blocks, offsets))
    return running


def halving_start(partial, axis_name, axis):
    count = lax.axis_size(axis_name)
    bits = count.bit_length() - 1
    shape = partial.shape
    block = shape[axis] // count
    value = partial.reshape(shape[:axis] + (2,) * bits + (block,) + shape[axis + 1 :])
    return (value, axis, tuple(range(bits - 1, -1, -1)))


def halving_step(state, axis_name, bit):
    value, axis, left = state
    count = lax.axis_size(axis_name)
    place = axis + left.index(bit)
    left = tuple(other for other in left if other != bit)
    mine = (lax.axis_index(axis_name) >> bit) & 1
    pairs = [(i, i ^ (1 << bit)) for i in range(count)]
    away = lax.dynamic_index_in_dim(value, 1 - mine, place, keepdims=False)
    arrived = lax.ppermute(away, axis_name, pairs)
    kept = lax.dynamic_index_in_dim(value, mine, place, keepdims=False)
    value = kept.astype(jnp.float32) + arrived.astype(jnp.float32)
    if left:
        value = value.astype(jnp.bfloat16)
    return (value, axis, left)


def halving_sum(partial, axis_name, axis, bit_order):
    count = lax.axis_size(axis_name)
    if count & (count - 1):
        owned = lax.psum_scatter(partial, axis_name, scatter_dimension=axis, tiled=True)
        return owned.astype(jnp.float32)
    state = halving_start(partial, axis_name, axis)
    for bit in bit_order:
        state = halving_step(state, axis_name, bit)
    return state[0].astype(jnp.float32)


def orders_of(count):
    bits = tuple(range(count.bit_length() - 1))
    first, second, rest = bits[:1], bits[1:2], bits[2:]
    return (bits, second + rest + first, rest[:1] + first + second + rest[1:])


def core_gradient(features, columns):
    width = features.shape[1]
    if lax.axis_size("batch") != 2:
        whole = lax.dot_general(
            features, columns, (((0,), (0,)), ((), ())), preferred_element_type=jnp.float32
        ).astype(jnp.bfloat16)
        return halving_sum(
            whole, "batch", 0, tuple(range(lax.axis_size("batch").bit_length() - 1))
        ).astype(jnp.bfloat16)
    core = lax.axis_index("batch")

    def rows_of(which):
        part = lax.dynamic_slice_in_dim(features, which * (width // 2), width // 2, 1)
        return lax.dot_general(
            part, columns, (((0,), (0,)), ((), ())), preferred_element_type=jnp.float32
        ).astype(jnp.bfloat16)

    arrived = lax.ppermute(rows_of(1 - core), "batch", [(0, 1), (1, 0)])
    kept = rows_of(core)
    return (kept.astype(jnp.float32) + arrived.astype(jnp.float32)).astype(jnp.bfloat16)


def weight_gradient(features, columns, order):
    return halving_sum(core_gradient(features, columns), "ctx", 0, order)


def route_gates(normed_rows, router_low, route_rows):
    logits = jnp.dot(normed_rows, router_low, preferred_element_type=jnp.float32)
    selection = (
        route_rows[:, :, None] == jnp.arange(EXPERTS, dtype=jnp.int32)[None, None, :]
    ).astype(jnp.float32)
    chosen = jnp.sum(selection * logits[:, None, :], axis=-1)
    shares = jax.nn.softmax(chosen, axis=-1)
    gate_table = jnp.sum(shares[:, :, None] * selection, axis=1)
    return (selection, shares, gate_table)


def swiglu_back(grad_active, gate_part, up_part):
    sigmoid_gate = jax.nn.sigmoid(gate_part)
    grad_gate = grad_active * up_part * sigmoid_gate * (1.0 + gate_part * (1.0 - sigmoid_gate))
    grad_up = grad_active * gate_part * sigmoid_gate
    return (grad_gate, grad_up)


def dot_t(left, right):
    return lax.dot_general(
        left, right, (((1,), (1,)), ((), ())), preferred_element_type=jnp.float32
    )


def adamw_step(weight, gradient, moment, second, step_rate, decay_rate):
    moment_new = BETA_ONE * moment + (1.0 - BETA_ONE) * gradient
    second_new = BETA_TWO * second + (1.0 - BETA_TWO) * gradient * gradient
    moment_hat = moment_new / (1.0 - BETA_ONE**STEP)
    second_hat = second_new / (1.0 - BETA_TWO**STEP)
    weight_new = weight - step_rate * (
        moment_hat / (jnp.sqrt(second_hat) + EPS_ADAM) + decay_rate * weight
    )
    return (moment_new, second_new, weight_new)


def body(
    inputs,
    cotangent,
    routes,
    segments,
    gains,
    gains_first,
    gains_second,
    w_query,
    query_first,
    query_second,
    w_keyvalue,
    keyvalue_first,
    keyvalue_second,
    w_out,
    out_first,
    out_second,
    w_router,
    router_first,
    router_second,
    w_gate_up,
    gate_up_first,
    gate_up_second,
    w_down,
    down_first,
    down_second,
):
    micro_count, unused, span_rows, width = inputs.shape
    rows = micro_count * span_rows
    kv_width = KV_HEADS * HEAD_DIM
    q_width = HEADS * HEAD_DIM
    group_size = HEADS // KV_HEADS
    ctx_count = lax.axis_size("ctx")
    order_a, order_b, order_c = orders_of(ctx_count)
    anchor = lax.axis_index("ctx") * span_rows
    cosine_table, sine_table = rope_tables(anchor + jnp.arange(span_rows, dtype=jnp.int32))
    cosine_table = jnp.tile(cosine_table, (micro_count, 1))
    sine_table = jnp.tile(sine_table, (micro_count, 1))
    weights = (gains, w_query, w_keyvalue, w_out, w_router, w_gate_up, w_down)
    firsts = (
        gains_first,
        query_first,
        keyvalue_first,
        out_first,
        router_first,
        gate_up_first,
        down_first,
    )
    seconds = (
        gains_second,
        query_second,
        keyvalue_second,
        out_second,
        router_second,
        gate_up_second,
        down_second,
    )
    everyone = ("batch", "ctx")
    own_rows = w_query.shape[0]
    dense_pack = jnp.concatenate(
        [
            w_query,
            w_keyvalue,
            w_out,
            w_router,
            gains.T,
            jnp.zeros((own_rows, 128 - EXPERTS - 2), jnp.float32),
        ],
        axis=1,
    ).astype(jnp.bfloat16)
    dense_all = lax.all_gather(dense_pack, everyone, axis=0, tiled=True)
    gate_up_flat = jnp.transpose(w_gate_up.astype(jnp.bfloat16), (1, 0, 2)).reshape(own_rows, -1)
    down_flat = jnp.transpose(w_down.astype(jnp.bfloat16), (1, 0, 2)).reshape(own_rows, -1)

    down_flat, dense_all = lax.optimization_barrier((down_flat, dense_all))
    down_low = lax.all_gather(down_flat, everyone, axis=0, tiled=True)
    qkv_low = dense_all[:, : q_width + 2 * kv_width]
    out_low = dense_all[:, q_width + 2 * kv_width : 2 * q_width + 2 * kv_width]
    tail = dense_all[:, 2 * q_width + 2 * kv_width :]
    router_low = tail[:, :EXPERTS]
    gain_attn = tail[:, EXPERTS].astype(jnp.float32)
    gain_ffn = tail[:, EXPERTS + 1].astype(jnp.float32)

    tokens = inputs.reshape(rows, width).astype(jnp.float32)
    cot_rows = cotangent.reshape(rows, width)
    route_rows = lax.dynamic_slice_in_dim(routes[:, 0], anchor, span_rows, 1).reshape(rows, -1)

    inv_first = lax.rsqrt(jnp.mean(tokens * tokens, axis=-1, keepdims=True) + EPS_NORM)
    unit_first = tokens * inv_first
    normed = (unit_first * gain_attn).astype(jnp.bfloat16)
    raw = jnp.dot(normed, qkv_low, preferred_element_type=jnp.float32)
    queries = rotate(
        raw[:, :q_width].reshape(rows, HEADS, HEAD_DIM), cosine_table, sine_table
    ).astype(jnp.bfloat16)
    key_rows = rotate(
        raw[:, q_width : q_width + kv_width].reshape(rows, KV_HEADS, HEAD_DIM),
        cosine_table,
        sine_table,
    ).astype(jnp.bfloat16)
    shipped = jnp.concatenate(
        [key_rows.reshape(rows, kv_width), raw[:, q_width + kv_width :].astype(jnp.bfloat16)],
        axis=1,
    ).reshape(micro_count, span_rows, 2 * kv_width)
    shipped, down_low = lax.optimization_barrier((shipped, down_low))
    shipped_all = lax.all_gather(shipped, "ctx", axis=1, tiled=True)
    gate_up_flat, shipped_all = lax.optimization_barrier((gate_up_flat, shipped_all))
    gate_up_low = lax.all_gather(gate_up_flat, everyone, axis=0, tiled=True)

    grouped = queries.reshape(micro_count, span_rows, KV_HEADS, group_size, HEAD_DIM)
    query_pos = anchor + jnp.arange(span_rows, dtype=jnp.int32)
    limit = anchor + span_rows
    attended_list = []
    log_list = []
    for micro_index in range(micro_count):
        segment_row = segments[micro_index, 0]
        maxima, totals, accumulated = fold_forward(
            (
                jnp.full((KV_HEADS, group_size, span_rows), MASKED, jnp.float32),
                jnp.zeros((KV_HEADS, group_size, span_rows), jnp.float32),
                jnp.zeros((span_rows, KV_HEADS, group_size, HEAD_DIM), jnp.float32),
            ),
            shipped_all[micro_index],
            grouped[micro_index],
            lax.dynamic_slice_in_dim(segment_row, anchor, span_rows),
            query_pos,
            segment_row,
            limit,
        )
        attended_list.append(
            (accumulated / jnp.transpose(totals, (2, 0, 1))[..., None]).reshape(span_rows, q_width)
        )
        log_list.append(maxima + jnp.log(totals))
    attended = jnp.concatenate(attended_list, axis=0)
    attended_low = attended.astype(jnp.bfloat16)
    middle = tokens + dot_t(attended_low, out_low)
    inv_second = lax.rsqrt(jnp.mean(middle * middle, axis=-1, keepdims=True) + EPS_NORM)
    unit_second = middle * inv_second
    normed_ffn = (unit_second * gain_ffn).astype(jnp.bfloat16)

    selection, shares, gate_table = route_gates(normed_ffn, router_low, route_rows)
    gate_and_up = jnp.dot(normed_ffn, gate_up_low, preferred_element_type=jnp.float32).reshape(
        rows, EXPERTS, 2 * FF
    )
    gate_part, up_part = gate_and_up[..., :FF], gate_and_up[..., FF:]
    active = jax.nn.silu(gate_part) * up_part
    scaled = (gate_table[:, :, None] * active).astype(jnp.bfloat16).reshape(rows, EXPERTS * FF)
    outputs = (middle + dot_t(scaled, down_low)).astype(jnp.bfloat16).reshape(inputs.shape)
    down_half = core_gradient(cot_rows, scaled)

    grad_scaled = jnp.dot(cot_rows, down_low, preferred_element_type=jnp.float32).reshape(
        rows, EXPERTS, FF
    )
    grad_gate_table = jnp.sum(grad_scaled * active, axis=-1)
    grad_gate, grad_up = swiglu_back(gate_table[:, :, None] * grad_scaled, gate_part, up_part)
    grad_both = (
        jnp.concatenate([grad_gate, grad_up], axis=-1)
        .astype(jnp.bfloat16)
        .reshape(rows, EXPERTS * 2 * FF)
    )
    middle_column = EXPERTS * FF
    halves = (
        core_gradient(normed_ffn, grad_both[:, :middle_column]),
        core_gradient(normed_ffn, grad_both[:, middle_column:]),
        down_half,
    )
    grad_normed_part = dot_t(grad_both, gate_up_low)
    orders = (order_a, order_b, order_c)
    stepwise = ctx_count & (ctx_count - 1) == 0
    grad_normed_part, halves = lax.optimization_barrier((grad_normed_part, halves))
    if stepwise:
        states = [halving_start(half, "ctx", 0) for half in halves]
    done_steps = 0

    grad_shares = jnp.sum(grad_gate_table[:, None, :] * selection, axis=-1)
    grad_chosen = shares * (grad_shares - jnp.sum(shares * grad_shares, axis=-1, keepdims=True))
    grad_logits = jnp.sum(grad_chosen[:, :, None] * selection, axis=1)
    grad_normed_ffn = grad_normed_part + jnp.dot(
        grad_logits, router_low.astype(jnp.float32).T, precision=HIGHEST
    )
    grad_router = jnp.dot(normed_ffn.astype(jnp.float32).T, grad_logits, precision=HIGHEST)
    scaled_ffn = grad_normed_ffn * gain_ffn
    grad_gain_ffn = jnp.sum(grad_normed_ffn * unit_second, axis=0)
    grad_middle = cot_rows.astype(jnp.float32) + inv_second * (
        scaled_ffn - unit_second * jnp.mean(scaled_ffn * unit_second, axis=-1, keepdims=True)
    )
    grad_branch = grad_middle.astype(jnp.bfloat16)
    grad_attended = jnp.dot(grad_branch, out_low, preferred_element_type=jnp.float32).astype(
        jnp.bfloat16
    )
    grad_grouped = grad_attended.reshape(micro_count, span_rows, KV_HEADS, group_size, HEAD_DIM)
    deltas = jnp.sum(
        (grad_attended.astype(jnp.float32) * attended).reshape(
            micro_count, span_rows, KV_HEADS, group_size, HEAD_DIM
        ),
        axis=-1,
    )
    grad_query_list = []
    grad_keys_list = []
    for micro_index in range(micro_count):
        segment_row = segments[micro_index, 0]
        grad_query_rot, grad_keys_all = fold_backward(
            (
                jnp.zeros((span_rows, KV_HEADS, group_size, HEAD_DIM), jnp.float32),
                jnp.zeros((segment_row.shape[0], 2 * kv_width), jnp.float32),
            ),
            shipped_all[micro_index],
            grouped[micro_index],
            grad_grouped[micro_index],
            log_list[micro_index],
            jnp.transpose(deltas[micro_index], (1, 2, 0)),
            lax.dynamic_slice_in_dim(segment_row, anchor, span_rows),
            query_pos,
            segment_row,
            limit,
        )
        if stepwise and done_steps < len(order_a) - 1:
            states = [
                halving_step(state, "ctx", order[done_steps])
                for state, order in zip(states, orders)
            ]
            done_steps += 1
            held, grad_query_rot, grad_keys_all, grad_grouped = lax.optimization_barrier(
                (tuple(state[0] for state in states), grad_query_rot, grad_keys_all, grad_grouped)
            )
            states = [(value,) + state[1:] for value, state in zip(held, states)]
        grad_query_list.append(grad_query_rot.reshape(span_rows, HEADS, HEAD_DIM))
        grad_keys_list.append(
            halving_sum(grad_keys_all.astype(jnp.bfloat16), "ctx", 0, (order_a, order_b)[micro_index % 2])
        )
    grad_shipped = jnp.concatenate(grad_keys_list, axis=0)
    grad_query_raw = rotate(
        jnp.concatenate(grad_query_list, axis=0), cosine_table, -sine_table
    ).reshape(rows, q_width)
    grad_key_raw = rotate(
        grad_shipped[:, :kv_width].reshape(rows, KV_HEADS, HEAD_DIM), cosine_table, -sine_table
    ).reshape(rows, kv_width)
    grad_raw = jnp.concatenate(
        [grad_query_raw, grad_key_raw, grad_shipped[:, kv_width:]], axis=1
    ).astype(jnp.bfloat16)
    grad_normed = dot_t(grad_raw, qkv_low)
    scaled_attn = grad_normed * gain_attn
    grad_gain_attn = jnp.sum(grad_normed * unit_first, axis=0)
    input_grads = (
        grad_middle
        + inv_first
        * (scaled_attn - unit_first * jnp.mean(scaled_attn * unit_first, axis=-1, keepdims=True))
    ).reshape(inputs.shape)
    out_owned = weight_gradient(grad_branch, attended_low, order_c)
    small = jnp.concatenate(
        [
            grad_router,
            grad_gain_attn[:, None],
            grad_gain_ffn[:, None],
            jnp.zeros((width, 128 - EXPERTS - 2), jnp.float32),
        ],
        axis=1,
    )
    if stepwise:
        owned_experts = []
        for state, order in zip(states, orders):
            for bit in order[done_steps:]:
                state = halving_step(state, "ctx", bit)
            owned_experts.append(state[0].astype(jnp.float32))
    else:
        owned_experts = [halving_sum(half, "ctx", 0, order_a) for half in halves]
    gate_up_owned = jnp.concatenate(owned_experts[:2], axis=1)
    down_owned = owned_experts[2]
    small_owned = lax.psum_scatter(small, everyone, scatter_dimension=0, tiled=True)
    raw_owned = weight_gradient(normed, grad_raw, order_a)
    owned_grads = (
        small_owned[:, EXPERTS : EXPERTS + 2].T,
        raw_owned[:, :q_width],
        raw_owned[:, q_width:],
        out_owned,
        small_owned[:, :EXPERTS],
        jnp.transpose(gate_up_owned.reshape(own_rows, EXPERTS, 2 * FF), (1, 0, 2)),
        jnp.transpose(down_owned.reshape(own_rows, EXPERTS, FF), (1, 0, 2)),
    )
    updated = []
    for kind_index in range(7):
        updated.extend(
            adamw_step(
                weights[kind_index],
                owned_grads[kind_index],
                firsts[kind_index],
                seconds[kind_index],
                RATES[kind_index],
                DECAYS[kind_index],
            )
        )
    (
        gains_moment,
        gains_square,
        gains_new,
        query_moment,
        query_square,
        query_new,
        keyvalue_moment,
        keyvalue_square,
        keyvalue_new,
        out_moment,
        out_square,
        out_new,
        router_moment,
        router_square,
        router_new,
        gate_up_moment,
        gate_up_square,
        gate_up_new,
        down_moment,
        down_square,
        down_new,
    ) = updated
    return (
        outputs,
        input_grads,
        gains_moment,
        gains_square,
        gains_new,
        query_moment,
        query_square,
        query_new,
        keyvalue_moment,
        keyvalue_square,
        keyvalue_new,
        out_moment,
        out_square,
        out_new,
        router_moment,
        router_square,
        router_new,
        gate_up_moment,
        gate_up_square,
        gate_up_new,
        down_moment,
        down_square,
        down_new,
    )


def solution(mesh):
    placed = (
        P(None, "batch", "ctx", None),
        P(None, "batch", "ctx", None),
        P(None, "batch", None, None),
        P(None, "batch", None),
        P(None, ("batch", "ctx")),
        P(None, ("batch", "ctx")),
        P(None, ("batch", "ctx")),
        P(("batch", "ctx"), None),
        P(("batch", "ctx"), None),
        P(("batch", "ctx"), None),
        P(("batch", "ctx"), None),
        P(("batch", "ctx"), None),
        P(("batch", "ctx"), None),
        P(("batch", "ctx"), None),
        P(("batch", "ctx"), None),
        P(("batch", "ctx"), None),
        P(("batch", "ctx"), None),
        P(("batch", "ctx"), None),
        P(("batch", "ctx"), None),
        P(None, ("batch", "ctx"), None),
        P(None, ("batch", "ctx"), None),
        P(None, ("batch", "ctx"), None),
        P(None, ("batch", "ctx"), None),
        P(None, ("batch", "ctx"), None),
        P(None, ("batch", "ctx"), None),
    )
    return jax.shard_map(
        body,
        mesh=mesh,
        in_specs=placed,
        out_specs=(
            P(None, "batch", "ctx", None),
            P(None, "batch", "ctx", None),
            P(None, ("batch", "ctx")),
            P(None, ("batch", "ctx")),
            P(None, ("batch", "ctx")),
            P(("batch", "ctx"), None),
            P(("batch", "ctx"), None),
            P(("batch", "ctx"), None),
            P(("batch", "ctx"), None),
            P(("batch", "ctx"), None),
            P(("batch", "ctx"), None),
            P(("batch", "ctx"), None),
            P(("batch", "ctx"), None),
            P(("batch", "ctx"), None),
            P(("batch", "ctx"), None),
            P(("batch", "ctx"), None),
            P(("batch", "ctx"), None),
            P(None, ("batch", "ctx"), None),
            P(None, ("batch", "ctx"), None),
            P(None, ("batch", "ctx"), None),
            P(None, ("batch", "ctx"), None),
            P(None, ("batch", "ctx"), None),
            P(None, ("batch", "ctx"), None),
        ),
        check_vma=False,
    )
```

time: 3960 us -> 1390 us (0.35)
  waiting for transfers between devices: 3170 us -> 737 us
  matrix products: 297 us -> 162 us
  blocking collectives: 129 us -> 0 us
  starting transfers between devices: 0.84 us -> 71.3 us
  other arithmetic: 81 us -> 122 us
    reduce_scatter x5 -> x0, waiting for transfers between devices: 2550 us -> none  [the longest x1 1400 us: body(): lax.psum_scatter(expert_sums[0], ('batch', 'ctx'), scatter_dimension=1, t...]
    ppermute x0 -> x33, waiting for transfers between devices: none -> 230 us  [the longest x28 229 us: halving_step(): arrived = lax.ppermute(away, axis_name, pairs)]
    dot_general x34 -> x20, matrix products: 266 us -> 119 us  [the longest x10 48 us: rows_of(): lax.dot_general(part, columns, (((0,), (0,)), ((), ())), preferred_elemen...]
    all_gather x2 -> x0, blocking collectives: 129 us -> none  [the longest x1 69.6 us: body(): lax.all_gather(w_router.astype(jnp.bfloat16), ('batch', 'ctx'), axis=0, t...]
    add x2 -> x0, local copies, waits for them, and re-layouts: 100 us -> none  [the longest x1 65.8 us: experts_backward(): sum_gate_up + jnp.einsum('cd,cef->edf', normed_ffn, grad_both, preferred_...]
    unnamed x20 -> x6, waiting for transfers between devices: 213 us -> 116 us
    ppermute x0 -> x33, starting transfers between devices: none -> 70.9 us  [the longest x28 69.8 us: halving_step(): arrived = lax.ppermute(away, axis_name, pairs)]
    all_gather x7 -> x4, waiting for transfers between devices: 405 us -> 391 us  [the longest x1 122 us: body(): gate_up_low = lax.all_gather(gate_up_flat, everyone, axis=0, tiled=True)]
  transfers between devices with their start and end apart: 16 -> 38, of which waited for: 13 -> 17; matrix products, arithmetic and copies ran while one was open for 11% -> 30% of each run, Pallas kernels for 0% -> 0%
where the time goes in v1:
time: 1390 us; the launch traced here: 1370 us
  waiting for transfers between devices  737 us (53%)
  local copies, waits for them, and re-layouts  241 us (17%)
  matrix products  162 us (12%)
  other arithmetic  122 us (9%)
  starting transfers between devices  71.3 us (5%)
  loops' own time  24.9 us (2%)
  between operations  15.9 us (1%)
    ppermute x28, waiting for transfers between devices, halving_step(): arrived = lax.ppermute(away, axis_name, pairs)  229 us
    all_gather x1, waiting for transfers between devices, body(): gate_up_low = lax.all_gather(gate_up_flat, everyone, axis=0, tiled=True)  122 us
    unnamed x6, waiting for transfers between devices  116 us
    all_gather x1, waiting for transfers between devices, body(): down_low = lax.all_gather(down_flat, everyone, axis=0, tiled=True)  107 us
    all_gather x1, waiting for transfers between devices, body(): shipped_all = lax.all_gather(shipped, 'ctx', axis=1, tiled=True)  92.9 us
    unnamed x196, local copies, waits for them, and re-layouts  77.5 us
    ppermute x28, starting transfers between devices, halving_step(): arrived = lax.ppermute(away, axis_name, pairs)  69.8 us
    all_gather x1, waiting for transfers between devices, body(): dense_all = lax.all_gather(dense_pack, everyone, axis=0, tiled=True)  69.5 us
  transfers between devices with their start and end apart: 38, of which 17 were waited for; matrix products, arithmetic and copies ran while one was open for 30% of the time, Pallas kernels for 0%

profile of v1, /device:TPU:10, one launch (start us, length us, event | category | flops | bytes accessed | tf_op | source)
XLA Modules:
  0.0 1374.1 jit_solution(7116759214654556848)
XLA Ops:
  14.6 69.5 %all-gather.5.cloned.1.call-done = bf16[1024,3200]{1,0:T(8,128)(2,1)} async-done(((bf16[32,3200]{1,0:T(8,128)(2,1)}), bf16[1024,3200]{1,0:T(8,128)(2,1)}) %all-gather.5.cloned.1.call-update) | async-done | bytes 6553616 | tf_op jit(solution)/shard_map/all_gather | solution.py:337
  93.4 106.6 %all-gather.7.cloned.1.call-done = bf16[1024,8192]{1,0:T(8,128)(2,1)} async-done(((bf16[32,8192]{1,0:T(8,128)(2,1)}), bf16[1024,8192]{1,0:T(8,128)(2,1)}) %all-gather.7.cloned.1.call-update) | async-done | bytes 16777232 | tf_op jit(solution)/shard_map/all_gather | solution.py:342
  203.4 92.9 %all-gather.9.cloned.1.call-done = bf16[2,1536,1024]{2,0,1:T(2,128)(2,1)} async-done(((bf16[2,96,1024]{2,0,1:T(2,128)(2,1)}), bf16[2,1536,1024]{2,0,1:T(2,128)(2,1)}) %all-gather.9.cloned.1.call-update) | async-done | bytes 6291472 | tf_op jit(solution)/shard_map/all_gather | solution.py:371
  297.6 7.6 fusion.178
  305.2 8.2 copy.447
  318.9 4.7 copy.369
  323.6 18.5 %while.57 = (s32[]{:T(128)}, f32[8,2,96]{2,1,0:T(2,128)S(1)}, f32[8,2,96]{2,1,0:T(2,128)S(1)}, f32[96,8,2,64]{0,3,2,1:T(8,128)S(1)}, s32[3]{0:T(128)S(1)}, /*ind...) while((s32[]{:T(128)}, f32[8,2,96]{2,1,0:T(2,128)S(1)}, ...), condition=%wide.region_12.13_spmd.clone, body=%wide.region_7.12_spmd.clone.sunk | while | flops 211899488 | bytes 15970521 | solution.py:98
  325.3 7.1 conditional.13
  333.6 7.1 conditional.13
  342.3 4.7 copy.367
  347.1 18.1 %while.56 = (s32[]{:T(128)}, f32[8,2,96]{2,1,0:T(2,128)S(1)}, f32[8,2,96]{2,1,0:T(2,128)S(1)}, f32[96,8,2,64]{0,3,2,1:T(8,128)S(1)}, s32[3]{0:T(128)S(1)}, /*ind...) while((s32[]{:T(128)}, f32[8,2,96]{2,1,0:T(2,128)S(1)}, ...), condition=%wide.region_6.7_spmd.clone, body=%wide.region_1.6_spmd.clone.sunk | while | flops 211899488 | bytes 15970521 | solution.py:98
  348.4 7.1 conditional.12
  356.8 7.1 conditional.12
  369.5 122.0 %all-gather.11.cloned.1.call-done = bf16[1024,16384]{1,0:T(8,128)(2,1)} async-done(((bf16[32,16384]{1,0:T(8,128)(2,1)}), bf16[1024,16384]{1,0:T(8,128)(2,1)}) %all-gather.11.cloned.1.call-update) | async-done | bytes 33554448 | tf_op jit(solution)/shard_map/all_gather | solution.py:373
  491.5 17.5 %fusion.175 = f32[192,16384]{1,0:T(8,128)} fusion(bf16[192,1024]{1,0:T(8,128)(2,1)S(1)} %multiply_convert_fusion.3, bf16[1024,16384]{1,0:T(8,128)(2,1)} %all-gather.11.cloned.1.call-done), kind=kOutput, calls=%fused_computation.366 | convolution fusion | flops 6442450944 | bytes 46530560 | tf_op jit(solution)/shard_map/dot_general | solution.py:407
  509.0 21.2 %copy.445 = f32[24,8,16,1024]{3,2,1,0:T(8,128)} copy(f32[24,8,16,1024]{3,1,2,0:T(8,128)} %bitcast.535) | data formatting | bytes 25165824
  530.2 7.4 multiply_reduce_fusion
  538.0 11.4 multiply_convert_fusion.1
  549.4 4.0 pad_maximum_fusion
  553.4 4.4 copy.448
  557.8 5.7 convolution_convert_fusion.4
  563.8 5.7 convolution_convert_fusion.2
  572.3 5.7 convolution_convert_fusion
  581.1 13.1 fusion.104
  594.3 18.2 %fusion.176 = f32[192,1024]{1,0:T(8,128)} fusion(bf16[192,16384]{1,0:T(8,128)(2,1)} %bitcast.528, bf16[1024,16384]{1,0:T(8,128)(2,1)} %all-gather.11.cloned.1.call-done), kind=kOutput, calls=%fused_computation.367 | convolution fusion | flops 6442450944 | bytes 40632320 | tf_op jit(solution)/shard_map/dot_general | solution.py:251
  612.5 10.1 add_convert_fusion.2
  622.6 6.9 add_convert_fusion.1
  629.5 9.2 add_convert_fusion
  643.0 6.3 constant_dynamic-slice_fusion.13
  664.4 6.0 collective-permute-done.23
  673.1 6.2 constant_dynamic-slice_fusion.9
  679.3 70.8 %collective-permute-done.24 = bf16[2,2,32,1024]{3,2,0,1:T(8,128)(2,1)S(1)} collective-permute-done((bf16[2,2,32,1024]{3,2,0,1:T(8,128)(2,1)S(1)}, bf16[2,2,32,1024]{3,2,0,1:T(8,128)(2,1)S(1)}, u32[]{:S(2)}, u32[]{:S(2)}) %collective-permute-start.24) | collective-permute-done | bytes 262176 | tf_op jit(solution)/shard_map/ppermute | solution.py:181
  769.9 57.8 %while.58 = (s32[]{:T(128)}, f32[96,8,2,64]{0,3,2,1:T(8,128)S(1)}, f32[1536,1024]{0,1:T(8,128)}, s32[3]{0:T(128)S(1)}, s32[]{:T(128)}, /*index=5*/s32[96]{0:T(12...) while((s32[]{:T(128)}, f32[96,8,2,64]{0,3,2,1:T(8,128)S(1)}, ...), condition=%wide.region_27.28_spmd.clone, body=%wide.region_24.27_spmd.clone.sunk | while | flops 514409056 | bytes 46840080 | solution.py:160
  771.1 27.1 %conditional.14 = ((f32[96,8,2,64]{0,3,2,1:T(8,128)S(1)}, f32[1536,1024]{0,1:T(8,128)})) conditional(s32[]{:T(128)} %convert_element_type.850, (f32[96,8,2,64]{0,3,2,1:T(8,128)S(1)}, f32[1536,1024]{0,1:T(8,128)}) %tuple.233, (s32[96]{0:T(128)S(1)}, s32[]{:T(128)}, s32[1536]{0:T(1024)S(1)}, s32[]{:T(128)}, bf16[3,512,1024]{1,2,0:T(8,128)(2,1)}, ...), branch_computations={%region_25.25_spmd, %region_26.26_spmd} | conditional | flops 514409056 | bytes 46839408 | solution.py:158
  787.6 10.6 dynamic_update_slice.6
  799.4 27.0 %conditional.14 = ((f32[96,8,2,64]{0,3,2,1:T(8,128)S(1)}, f32[1536,1024]{0,1:T(8,128)})) conditional(s32[]{:T(128)} %convert_element_type.850, (f32[96,8,2,64]{0,3,2,1:T(8,128)S(1)}, f32[1536,1024]{0,1:T(8,128)}) %tuple.233, (s32[96]{0:T(128)S(1)}, s32[]{:T(128)}, s32[1536]{0:T(1024)S(1)}, s32[]{:T(128)}, bf16[3,512,1024]{1,2,0:T(8,128)(2,1)}, ...), branch_computations={%region_25.25_spmd, %region_26.26_spmd} | conditional | flops 514409056 | bytes 46839408 | solution.py:158
  815.9 10.5 dynamic_update_slice.6
  827.7 24.9 %collective-permute-done.26 = bf16[32,1024]{1,0:T(8,128)(2,1)} collective-permute-done((bf16[32,1024]{1,0:T(8,128)(2,1)}, bf16[32,1024]{1,0:T(8,128)(2,1)}, u32[]{:S(2)}, u32[]{:S(2)}) %collective-permute-start.26) | collective-permute-done | bytes 65568 | tf_op jit(solution)/shard_map/ppermute | solution.py:181
  854.5 5.2 fusion.72
  859.7 7.2 fusion.71
  866.9 5.7 fusion.70
  875.5 5.4 copy.386
  880.9 3.6 constant_dynamic-slice_fusion.7
  896.8 59.1 %while.59 = (s32[]{:T(128)}, f32[96,8,2,64]{0,3,2,1:T(8,128)S(1)}, f32[1536,1024]{0,1:T(8,128)}, s32[3]{0:T(128)S(1)}, s32[]{:T(128)}, /*index=5*/s32[96]{0:T(12...) while((s32[]{:T(128)}, f32[96,8,2,64]{0,3,2,1:T(8,128)S(1)}, ...), condition=%wide.region_31.32_spmd.clone, body=%wide.region_28.31_spmd.clone.sunk | while | flops 514409056 | bytes 46840080 | solution.py:160
  898.2 27.6 %conditional.15 = ((f32[96,8,2,64]{0,3,2,1:T(8,128)S(1)}, f32[1536,1024]{0,1:T(8,128)})) conditional(s32[]{:T(128)} %convert_element_type.851, (f32[96,8,2,64]{0,3,2,1:T(8,128)S(1)}, f32[1536,1024]{0,1:T(8,128)}) %tuple.236, (s32[96]{0:T(128)S(1)}, s32[]{:T(128)}, s32[1536]{0:T(1024)}, s32[]{:T(128)}, bf16[3,512,1024]{1,2,0:T(8,128)(2,1)}, ...), branch_computations={%region_29.29_spmd, %region_30.30_spmd} | conditional | flops 514409056 | bytes 46839408 | solution.py:158
  915.3 10.6 dynamic_update_slice.7
  927.1 27.5 %conditional.15 = ((f32[96,8,2,64]{0,3,2,1:T(8,128)S(1)}, f32[1536,1024]{0,1:T(8,128)})) conditional(s32[]{:T(128)} %convert_element_type.851, (f32[96,8,2,64]{0,3,2,1:T(8,128)S(1)}, f32[1536,1024]{0,1:T(8,128)}) %tuple.236, (s32[96]{0:T(128)S(1)}, s32[]{:T(128)}, s32[1536]{0:T(1024)}, s32[]{:T(128)}, bf16[3,512,1024]{1,2,0:T(8,128)(2,1)}, ...), branch_computations={%region_29.29_spmd, %region_30.30_spmd} | conditional | flops 514409056 | bytes 46839408 | solution.py:158
  944.1 10.5 dynamic_update_slice.7
  955.9 3.9 copy.388
  968.8 3.6 fusion.76
  975.9 5.4 copy.391
  981.3 4.0 constant_dynamic-slice_fusion.5
  986.1 3.7 copy.438
  992.1 28.8 %collective-permute-start.29 = (bf16[2,32,8192]{2,1,0:T(8,128)(2,1)}, bf16[2,32,8192]{2,1,0:T(8,128)(2,1)}, u32[]{:S(2)}, u32[]{:S(2)}) collective-permute-start(bf16[2,32,8192]{2,1,0:T(8,128)(2,1)} %dynamic-slice_bitcast_fusion.10), channel_id=1, source_target_pairs={{0,8},{1,9},{2,10},{3,11},{4,12},{5,13},{6,14},{7,15},{8,0},{9,1},... | collective-permute-start | bytes 3145736 | tf_op jit(solution)/shard_map/ppermute | solution.py:181
  1029.7 46.6 %collective-permute-done.11 = bf16[2,96,1024]{1,2,0:T(8,128)(2,1)S(1)} collective-permute-done((bf16[2,96,1024]{1,2,0:T(8,128)(2,1)S(1)}, bf16[2,96,1024]{1,2,0:T(8,128)(2,1)S(1)}, u32[]{:S(2)}, u32[]{:S(2)}) %collective-permute-start.11) | collective-permute-done | bytes 393248 | tf_op jit(solution)/shard_map/ppermute | solution.py:181
  1080.4 6.1 collective-permute-done.12
  1097.5 3.7 copy.393
  1111.5 33.3 %collective-permute-done.14 = bf16[2,2,96,1024]{3,2,1,0:T(8,128)(2,1)} collective-permute-done((bf16[2,2,96,1024]{3,2,1,0:T(8,128)(2,1)S(1)}, bf16[2,2,96,1024]{3,2,1,0:T(8,128)(2,1)}, u32[]{:S(2)}, u32[]{:S(2)}) %collective-permute-start.14) | collective-permute-done | bytes 786464 | tf_op jit(solution)/shard_map/ppermute | solution.py:181
  1152.6 21.2 %collective-permute-done.15 = bf16[2,96,1024]{1,2,0:T(8,128)(2,1)S(1)} collective-permute-done((bf16[2,96,1024]{1,2,0:T(8,128)(2,1)S(1)}, bf16[2,96,1024]{1,2,0:T(8,128)(2,1)S(1)}, u32[]{:S(2)}, u32[]{:S(2)}) %collective-permute-start.15) | collective-permute-done | bytes 393248 | tf_op jit(solution)/shard_map/ppermute | solution.py:181
  1175.9 6.4 collective-permute-done.16
  1191.5 4.6 multiply_subtract_fusion
  1221.5 7.6 collective-permute-done.19
  1236.1 115.8 %reduce-scatter.4.cloned.1.call-done = f32[32,128]{1,0:T(8,128)} async-done(((f32[1024,128]{1,0:T(8,128)}), f32[32,128]{1,0:T(8,128)}) %reduce-scatter.4.cloned.1.call-update) | async-done | bytes 16400
  1355.3 5.4 collective-permute-start.21
  (559 shorter events, 293.4 us)
Async XLA Ops:
  7.2 289.4 %copy-start = (s32[2,1,1536,8]{2,3,1,0:T(8,128)S(1)}, s32[2,1,1536,8]{2,3,1,0:T(8,128)}, u32[]{:S(2)}) copy-start(s32[2,1,1536,8]{2,3,1,0:T(8,128)} %param.43) | copy-start | bytes 294916
  7.2 77.0 %copy-start.37 = (bf16[2,1,96,1024]{3,2,1,0:T(8,128)(2,1)S(1)}, bf16[2,1,96,1024]{3,2,1,0:T(8,128)(2,1)}, u32[]{:S(2)}) copy-start(bf16[2,1,96,1024]{3,2,1,0:T(8,128)(2,1)} %param.41) | copy-start | bytes 1179652
  7.2 76.9 %all-gather.5.cloned.1.call-start = ((), (), s32[]{:S(2)}) async-start(), calls=%async_computation.1 | async-start | bytes 6758400 | tf_op jit(solution)/shard_map/all_gather | solution.py:337
  12.4 187.5 %all-gather.7.cloned.1.call-start = ((), (), s32[]{:S(2)}) async-start(), calls=%async_computation.2 | async-start | bytes 17301504 | tf_op jit(solution)/shard_map/all_gather | solution.py:342
  84.1 212.2 %all-gather.9.cloned.1.call-start = ((), (), s32[]{:S(2)}) async-start(), calls=%async_computation.3 | async-start | bytes 6684672 | tf_op jit(solution)/shard_map/all_gather | solution.py:371
  84.8 212.4 %copy-start.53 = (f32[192,32]{0,1:T(8,128)}, f32[192,32]{0,1:T(8,128)S(1)}, u32[]{:S(2)}) copy-start(f32[192,32]{0,1:T(8,128)S(1)} %tile.18) | copy-start | bytes 73732
  86.3 554.7 %copy-start.65 = (f32[1024]{0:T(1024)}, f32[1024]{0:T(1024)S(1)}, u32[]{:S(2)}) copy-start(f32[1024]{0:T(1024)S(1)} %get-tuple-element.1183) | copy-start | bytes 12292
  91.8 110.4 %copy-start.22 = (f32[16,32,1024]{2,1,0:T(8,128)S(1)}, f32[16,32,1024]{2,1,0:T(8,128)}, u32[]{:S(2)}) copy-start(f32[16,32,1024]{2,1,0:T(8,128)} %param.60) | copy-start | bytes 6291460
  202.1 94.7 %copy-start.76 = (s32[2,1,1536]{2,1,0:T(1,128)S(1)}, s32[2,1,1536]{2,1,0:T(1,128)}, u32[]{:S(2)}) copy-start(s32[2,1,1536]{2,1,0:T(1,128)} %param.44) | copy-start | bytes 36868
  202.1 289.3 %all-gather.11.cloned.1.call-start = ((), (), s32[]{:S(2)}) async-start(), calls=%async_computation.4 | async-start | bytes 34603008 | tf_op jit(solution)/shard_map/all_gather | solution.py:373
  202.4 94.5 %slice-start.2 = ((f32[192,2048]{1,0:T(8,128)}), f32[192,1024]{1,0:T(8,128)S(1)}, s32[]{:S(2)}) async-start(f32[192,2048]{1,0:T(8,128)} %copy-done.42), calls=%async_computation.8 | async-start | bytes 1572864 | tf_op jit(solution)/shard_map/slice | solution.py:359
  296.3 1055.6 %reduce-scatter.4.cloned.1.call-start = ((), (), s32[]{:S(2)}) async-start(), calls=%async_computation.5 | async-start | bytes 540672
  347.1 18.3 %copy-start.38 = (bf16[2,1,96,1024]{3,2,1,0:T(8,128)(2,1)S(1)}, bf16[2,1,96,1024]{3,2,1,0:T(8,128)(2,1)}, u32[]{:S(2)}) copy-start(bf16[2,1,96,1024]{3,2,1,0:T(8,128)(2,1)} %param.41) | copy-start | bytes 1179652
  368.0 273.0 %copy-start.16 = (f32[192,1024]{1,0:T(8,128)}, f32[192,1024]{1,0:T(8,128)S(1)}, u32[]{:S(2)}) copy-start(f32[192,1024]{1,0:T(8,128)S(1)} %get-tuple-element.1371) | copy-start | bytes 2359300
  368.0 273.0 %copy-start.73 = (f32[192]{0:T(256)}, f32[192]{0:T(256)S(1)}, u32[]{:S(2)}) copy-start(f32[192]{0:T(256)S(1)} %add_rsqrt_fusion) | copy-start | bytes 2308
  563.5 49.0 %collective-permute-start = (bf16[512,8192]{1,0:T(8,128)(2,1)}, bf16[512,8192]{1,0:T(8,128)(2,1)}, u32[]{:S(2)}, u32[]{:S(2)}) collective-permute-start(bf16[512,8192]{1,0:T(8,128)(2,1)} %convolution_convert_fusion.4), channel_id=1, source_target_pairs={{0,16},{16,0},{1,17},{17,1},{2,18},{18,2},{3,19},{19,3},{4,20},{20... | collective-permute-start | bytes 25165832 | tf_op jit(solution)/shard_map/ppermute | solution.py:223
  569.5 53.1 %collective-permute-start.1 = (bf16[512,8192]{1,0:T(8,128)(2,1)}, bf16[512,8192]{1,0:T(8,128)(2,1)}, u32[]{:S(2)}, u32[]{:S(2)}) collective-permute-start(bf16[512,8192]{1,0:T(8,128)(2,1)} %convolution_convert_fusion.2), channel_id=1, source_target_pairs={{0,16},{16,0},{1,17},{17,1},{2,18},{18,2},{3,19},{19,3},{4,20},{20... | collective-permute-start | bytes 25165832 | tf_op jit(solution)/shard_map/ppermute | solution.py:223
  578.1 51.4 %collective-permute-start.2 = (bf16[512,8192]{1,0:T(8,128)(2,1)}, bf16[512,8192]{1,0:T(8,128)(2,1)}, u32[]{:S(2)}, u32[]{:S(2)}) collective-permute-start(bf16[512,8192]{1,0:T(8,128)(2,1)} %convolution_convert_fusion), channel_id=1, source_target_pairs={{0,16},{16,0},{1,17},{17,1},{2,18},{18,2},{3,19},{19,3},{4,20},{20... | collective-permute-start | bytes 25165832 | tf_op jit(solution)/shard_map/ppermute | solution.py:223
  642.8 9.3 collective-permute-start.22
  651.5 203.0 %collective-permute-start.3 = (bf16[2,2,2,32,8192]{4,3,0,1,2:T(8,128)(2,1)}, bf16[2,2,2,32,8192]{4,3,0,1,2:T(8,128)(2,1)}, u32[]{:S(2)}, u32[]{:S(2)}) collective-permute-start(bf16[2,2,2,32,8192]{4,3,0,1,2:T(8,128)(2,1)} %bitcast.486), channel_id=1, source_target_pairs={{0,1},{1,0},{2,3},{3,2},{4,5},{5,4},{6,7},{7,6},{8,9},{9,8},{10,11... | collective-permute-start | bytes 12582920 | tf_op jit(solution)/shard_map/ppermute | solution.py:181
  655.6 14.8 %collective-permute-start.23 = (bf16[2,2,2,32,1024]{4,3,0,1,2:T(8,128)(2,1)}, bf16[2,2,2,32,1024]{4,3,0,1,2:T(8,128)(2,1)}, u32[]{:S(2)}, u32[]{:S(2)}) collective-permute-start(bf16[2,2,2,32,1024]{4,3,0,1,2:T(8,128)(2,1)} %bitcast.488), channel_id=1, source_target_pairs={{0,4},{1,5},{2,6},{3,7},{4,0},{5,1},{6,2},{7,3},{8,12},{9,13},{10,... | collective-permute-start | bytes 1572872 | tf_op jit(solution)/shard_map/ppermute | solution.py:181
  663.0 196.7 %collective-permute-start.4 = (bf16[2,2,2,32,8192]{4,3,2,0,1:T(8,128)(2,1)}, bf16[2,2,2,32,8192]{4,3,2,0,1:T(8,128)(2,1)}, u32[]{:S(2)}, u32[]{:S(2)}) collective-permute-start(bf16[2,2,2,32,8192]{4,3,2,0,1:T(8,128)(2,1)} %bitcast.485), channel_id=1, source_target_pairs={{0,2},{1,3},{2,0},{3,1},{4,6},{5,7},{6,4},{7,5},{8,10},{9,11},{10,... | collective-permute-start | bytes 12582920 | tf_op jit(solution)/shard_map/ppermute | solution.py:181
  671.6 78.5 %collective-permute-start.24 = (bf16[2,2,32,1024]{3,2,0,1:T(8,128)(2,1)S(1)}, bf16[2,2,32,1024]{3,2,0,1:T(8,128)(2,1)S(1)}, u32[]{:S(2)}, u32[]{:S(2)}) collective-permute-start(bf16[2,2,32,1024]{3,2,0,1:T(8,128)(2,1)S(1)} %dynamic-slice_bitcast_fusion.18), channel_id=1, source_target_pairs={{0,1},{1,0},{2,3},{3,2},{4,5},{5,4},{6,7},{7,6},{8,9},{9,8},{10,11... | collective-permute-start | bytes 786440 | tf_op jit(solution)/shard_map/ppermute | solution.py:181
  750.8 10.3 collective-permute-start.25
  757.3 109.7 %collective-permute-start.5 = (bf16[2,2,2,32,8192]{4,3,0,1,2:T(8,128)(2,1)}, bf16[2,2,2,32,8192]{4,3,0,1,2:T(8,128)(2,1)}, u32[]{:S(2)}, u32[]{:S(2)}) collective-permute-start(bf16[2,2,2,32,8192]{4,3,0,1,2:T(8,128)(2,1)} %bitcast.484), channel_id=1, source_target_pairs={{0,4},{1,5},{2,6},{3,7},{4,0},{5,1},{6,2},{7,3},{8,12},{9,13},{10,... | collective-permute-start | bytes 12582920 | tf_op jit(solution)/shard_map/ppermute | solution.py:181
  762.8 89.8 %collective-permute-start.26 = (bf16[32,1024]{1,0:T(8,128)(2,1)}, bf16[32,1024]{1,0:T(8,128)(2,1)}, u32[]{:S(2)}, u32[]{:S(2)}) collective-permute-start(bf16[32,1024]{1,0:T(8,128)(2,1)} %dynamic-slice_bitcast_fusion.24), channel_id=1, source_target_pairs={{0,8},{1,9},{2,10},{3,11},{4,12},{5,13},{6,14},{7,15},{8,0},{9,1},... | collective-permute-start | bytes 196616 | tf_op jit(solution)/shard_map/ppermute | solution.py:181
  874.1 92.0 %collective-permute-start.6 = (bf16[2,2,32,8192]{3,2,0,1:T(8,128)(2,1)}, bf16[2,2,32,8192]{3,2,0,1:T(8,128)(2,1)}, u32[]{:S(2)}, u32[]{:S(2)}) collective-permute-start(bf16[2,2,32,8192]{3,2,0,1:T(8,128)(2,1)} %dynamic-slice_bitcast_fusion.6), channel_id=1, source_target_pairs={{0,2},{1,3},{2,0},{3,1},{4,6},{5,7},{6,4},{7,5},{8,10},{9,11},{10,... | collective-permute-start | bytes 6291464 | tf_op jit(solution)/shard_map/ppermute | solution.py:181
  884.5 71.4 %collective-permute-start.9 = (bf16[2,2,2,96,1024]{4,3,2,1,0:T(8,128)(2,1)}, bf16[2,2,2,96,1024]{4,3,2,1,0:T(8,128)(2,1)}, u32[]{:S(2)}, u32[]{:S(2)}) collective-permute-start(bf16[2,2,2,96,1024]{4,3,2,1,0:T(8,128)(2,1)} %get-tuple-element.1342), channel_id=1, source_target_pairs={{0,1},{1,0},{2,3},{3,2},{4,5},{5,4},{6,7},{7,6},{8,9},{9,8},{10,11... | collective-permute-start | bytes 4718600 | tf_op jit(solution)/shard_map/ppermute | solution.py:181
  886.6 82.2 %collective-permute-start.7 = (bf16[2,2,32,8192]{3,2,1,0:T(8,128)(2,1)}, bf16[2,2,32,8192]{3,2,1,0:T(8,128)(2,1)}, u32[]{:S(2)}, u32[]{:S(2)}) collective-permute-start(bf16[2,2,32,8192]{3,2,1,0:T(8,128)(2,1)} %dynamic-slice_bitcast_fusion.5), channel_id=1, source_target_pairs={{0,4},{1,5},{2,6},{3,7},{4,0},{5,1},{6,2},{7,3},{8,12},{9,13},{10,... | collective-permute-start | bytes 6291464 | tf_op jit(solution)/shard_map/ppermute | solution.py:181
  888.9 83.5 %collective-permute-start.8 = (bf16[2,2,32,8192]{3,2,0,1:T(8,128)(2,1)}, bf16[2,2,32,8192]{3,2,0,1:T(8,128)(2,1)}, u32[]{:S(2)}, u32[]{:S(2)}) collective-permute-start(bf16[2,2,32,8192]{3,2,0,1:T(8,128)(2,1)} %dynamic-slice_bitcast_fusion.4), channel_id=1, source_target_pairs={{0,1},{1,0},{2,3},{3,2},{4,5},{5,4},{6,7},{7,6},{8,9},{9,8},{10,11... | collective-permute-start | bytes 6291464 | tf_op jit(solution)/shard_map/ppermute | solution.py:181
  964.6 58.5 %collective-permute-start.10 = (bf16[2,2,96,1024]{3,2,1,0:T(8,128)(2,1)}, bf16[2,2,96,1024]{3,2,1,0:T(8,128)(2,1)}, u32[]{:S(2)}, u32[]{:S(2)}) collective-permute-start(bf16[2,2,96,1024]{3,2,1,0:T(8,128)(2,1)} %bitcast.104), channel_id=1, source_target_pairs={{0,2},{1,3},{2,0},{3,1},{4,6},{5,7},{6,4},{7,5},{8,10},{9,11},{10,... | collective-permute-start | bytes 2359304 | tf_op jit(solution)/shard_map/ppermute | solution.py:181
  985.3 112.2 %collective-permute-start.13 = (bf16[2,2,2,96,1024]{4,3,2,1,0:T(8,128)(2,1)}, bf16[2,2,2,96,1024]{4,3,2,1,0:T(8,128)(2,1)}, u32[]{:S(2)}, u32[]{:S(2)}) collective-permute-start(bf16[2,2,2,96,1024]{4,3,2,1,0:T(8,128)(2,1)} %get-tuple-element.1344), channel_id=1, source_target_pairs={{0,2},{1,3},{2,0},{3,1},{4,6},{5,7},{6,4},{7,5},{8,10},{9,11},{10,... | collective-permute-start | bytes 4718600 | tf_op jit(solution)/shard_map/ppermute | solution.py:181
  992.1 94.5 %collective-permute-start.29 = (bf16[2,32,8192]{2,1,0:T(8,128)(2,1)}, bf16[2,32,8192]{2,1,0:T(8,128)(2,1)}, u32[]{:S(2)}, u32[]{:S(2)}) collective-permute-start(bf16[2,32,8192]{2,1,0:T(8,128)(2,1)} %dynamic-slice_bitcast_fusion.10), channel_id=1, source_target_pairs={{0,8},{1,9},{2,10},{3,11},{4,12},{5,13},{6,14},{7,15},{8,0},{9,1},... | collective-permute-start | bytes 3145736 | tf_op jit(solution)/shard_map/ppermute | solution.py:181
  1021.9 68.6 %collective-permute-start.27 = (bf16[2,32,8192]{2,1,0:T(8,128)(2,1)}, bf16[2,32,8192]{2,1,0:T(8,128)(2,1)}, u32[]{:S(2)}, u32[]{:S(2)}) collective-permute-start(bf16[2,32,8192]{2,1,0:T(8,128)(2,1)} %dynamic-slice_bitcast_fusion.11), channel_id=1, source_target_pairs={{0,4},{1,5},{2,6},{3,7},{4,0},{5,1},{6,2},{7,3},{8,12},{9,13},{10,... | collective-permute-start | bytes 3145736 | tf_op jit(solution)/shard_map/ppermute | solution.py:181
  1027.2 51.8 %copy-start.54 = (f32[192,32]{0,1:T(8,128)S(1)}, f32[192,32]{0,1:T(8,128)}, u32[]{:S(2)}) copy-start(f32[192,32]{0,1:T(8,128)} %copy-done.53) | copy-start | bytes 73732
  1027.3 51.8 %copy-start.63 = (f32[192,32]{0,1:T(8,128)S(1)}, f32[192,32]{0,1:T(8,128)}, u32[]{:S(2)}) copy-start(f32[192,32]{0,1:T(8,128)} %neg.22) | copy-start | bytes 73732
  1027.3 49.0 %collective-permute-start.11 = (bf16[2,96,1024]{1,2,0:T(8,128)(2,1)S(1)}, bf16[2,96,1024]{1,2,0:T(8,128)(2,1)S(1)}, u32[]{:S(2)}, u32[]{:S(2)}) collective-permute-start(bf16[2,96,1024]{1,2,0:T(8,128)(2,1)S(1)} %dynamic-slice_bitcast_fusion.17), channel_id=1, source_target_pairs={{0,4},{1,5},{2,6},{3,7},{4,0},{5,1},{6,2},{7,3},{8,12},{9,13},{10,... | collective-permute-start | bytes 1179656 | tf_op jit(solution)/shard_map/ppermute | solution.py:181
  1028.3 58.2 %copy-start.21 = (bf16[2,2,32,8192]{3,2,1,0:T(8,128)(2,1)S(1)}, bf16[2,2,32,8192]{3,2,1,0:T(8,128)(2,1)}, u32[]{:S(2)}) copy-start(bf16[2,2,32,8192]{3,2,1,0:T(8,128)(2,1)} %fusion.76) | copy-start | bytes 6291460
  1028.4 67.9 %collective-permute-start.31 = (bf16[2,32,8192]{2,1,0:T(8,128)(2,1)S(1)}, bf16[2,32,8192]{2,1,0:T(8,128)(2,1)S(1)}, u32[]{:S(2)}, u32[]{:S(2)}) collective-permute-start(bf16[2,32,8192]{2,1,0:T(8,128)(2,1)S(1)} %dynamic-slice_bitcast_fusion.9), channel_id=1, source_target_pairs={{0,2},{1,3},{2,0},{3,1},{4,6},{5,7},{6,4},{7,5},{8,10},{9,11},{10,... | collective-permute-start | bytes 3145736 | tf_op jit(solution)/shard_map/ppermute | solution.py:181
  1076.5 10.0 collective-permute-start.12
  1089.0 62.4 %collective-permute-start.30 = (bf16[32,8192]{1,0:T(8,128)(2,1)}, bf16[32,8192]{1,0:T(8,128)(2,1)}, u32[]{:S(2)}, u32[]{:S(2)}) collective-permute-start(bf16[32,8192]{1,0:T(8,128)(2,1)} %dynamic-slice_bitcast_fusion.13), channel_id=1, source_target_pairs={{0,1},{1,0},{2,3},{3,2},{4,5},{5,4},{6,7},{7,6},{8,9},{9,8},{10,11... | collective-permute-start | bytes 1572872 | tf_op jit(solution)/shard_map/ppermute | solution.py:181
  1092.9 81.8 %collective-permute-start.28 = (bf16[32,8192]{1,0:T(8,128)(2,1)}, bf16[32,8192]{1,0:T(8,128)(2,1)}, u32[]{:S(2)}, u32[]{:S(2)}) collective-permute-start(bf16[32,8192]{1,0:T(8,128)(2,1)} %dynamic-slice_bitcast_fusion.14), channel_id=1, source_target_pairs={{0,8},{1,9},{2,10},{3,11},{4,12},{5,13},{6,14},{7,15},{8,0},{9,1},... | collective-permute-start | bytes 1572872 | tf_op jit(solution)/shard_map/ppermute | solution.py:181
  1105.7 41.6 %copy-start.26 = (bf16[2,2,2,96,1024]{3,4,2,0,1:T(8,128)(2,1)S(1)}, bf16[2,2,2,96,1024]{3,4,2,0,1:T(8,128)(2,1)}, u32[]{:S(2)}) copy-start(bf16[2,2,2,96,1024]{3,4,2,0,1:T(8,128)(2,1)} %copy-done.25) | copy-start | bytes 4718596
  1107.3 37.5 %collective-permute-start.14 = (bf16[2,2,96,1024]{3,2,1,0:T(8,128)(2,1)S(1)}, bf16[2,2,96,1024]{3,2,1,0:T(8,128)(2,1)}, u32[]{:S(2)}, u32[]{:S(2)}) collective-permute-start(bf16[2,2,96,1024]{3,2,1,0:T(8,128)(2,1)S(1)} %bitcast.583), channel_id=1, source_target_pairs={{0,4},{1,5},{2,6},{3,7},{4,0},{5,1},{6,2},{7,3},{8,12},{9,13},{10,... | collective-permute-start | bytes 2359304 | tf_op jit(solution)/shard_map/ppermute | solution.py:181
  1109.3 75.8 %collective-permute-start.32 = (bf16[32,8192]{1,0:T(8,128)(2,1)}, bf16[32,8192]{1,0:T(8,128)(2,1)}, u32[]{:S(2)}, u32[]{:S(2)}) collective-permute-start(bf16[32,8192]{1,0:T(8,128)(2,1)} %dynamic-slice_bitcast_fusion.12), channel_id=1, source_target_pairs={{0,8},{1,9},{2,10},{3,11},{4,12},{5,13},{6,14},{7,15},{8,0},{9,1},... | collective-permute-start | bytes 1572872 | tf_op jit(solution)/shard_map/ppermute | solution.py:181
  1148.9 25.8 %copy-start.34 = (bf16[2,32,8192]{2,1,0:T(8,128)(2,1)S(1)}, bf16[2,32,8192]{2,1,0:T(8,128)(2,1)}, u32[]{:S(2)}) copy-start(bf16[2,32,8192]{2,1,0:T(8,128)(2,1)} %copy-done.33) | copy-start | bytes 3145732
  1149.0 24.9 %collective-permute-start.15 = (bf16[2,96,1024]{1,2,0:T(8,128)(2,1)S(1)}, bf16[2,96,1024]{1,2,0:T(8,128)(2,1)S(1)}, u32[]{:S(2)}, u32[]{:S(2)}) collective-permute-start(bf16[2,96,1024]{1,2,0:T(8,128)(2,1)S(1)} %dynamic-slice_bitcast_fusion.16), channel_id=1, source_target_pairs={{0,8},{1,9},{2,10},{3,11},{4,12},{5,13},{6,14},{7,15},{8,0},{9,1},... | collective-permute-start | bytes 1179656 | tf_op jit(solution)/shard_map/ppermute | solution.py:181
  1174.0 8.3 collective-permute-start.16
  1183.7 4.2 collective-permute-start.17
  1189.1 25.3 %collective-permute-start.18 = (bf16[2,2,2,32,2048]{4,3,0,1,2:T(8,128)(2,1)S(1)}, bf16[2,2,2,32,2048]{4,3,0,1,2:T(8,128)(2,1)S(1)}, u32[]{:S(2)}, u32[]{:S(2)}) collective-permute-start(bf16[2,2,2,32,2048]{4,3,0,1,2:T(8,128)(2,1)S(1)} %bitcast.580), channel_id=1, source_target_pairs={{0,1},{1,0},{2,3},{3,2},{4,5},{5,4},{6,7},{7,6},{8,9},{9,8},{10,11... | collective-permute-start | bytes 3145736 | tf_op jit(solution)/shard_map/ppermute | solution.py:181
  1215.6 13.5 collective-permute-start.19
  1218.4 15.3 %copy-start.66 = (f32[1024]{0:T(1024)S(1)}, f32[1024]{0:T(1024)}, u32[]{:S(2)}) copy-start(f32[1024]{0:T(1024)} %copy-done.65) | copy-start | bytes 12292
  1218.4 15.3 %copy-start.74 = (f32[192]{0:T(256)S(1)}, f32[192]{0:T(256)}, u32[]{:S(2)}) copy-start(f32[192]{0:T(256)} %copy-done.73) | copy-start | bytes 2308
  1218.4 15.3 %copy-start.78 = (f32[192]{0:T(256)S(1)}, f32[192]{0:T(256)}, u32[]{:S(2)}) copy-start(f32[192]{0:T(256)} %copy-done.77) | copy-start | bytes 2308
  1221.4 132.2 %copy-start.72 = (f32[32,16]{0,1:T(8,128)S(1)}, f32[32,16]{0,1:T(8,128)}, u32[]{:S(2)}) copy-start(f32[32,16]{0,1:T(8,128)} %param.57) | copy-start | bytes 6148
  1221.5 132.1 %copy-start.81 = (f32[32,16]{0,1:T(8,128)S(1)}, f32[32,16]{0,1:T(8,128)}, u32[]{:S(2)}) copy-start(f32[32,16]{0,1:T(8,128)} %param.59) | copy-start | bytes 6148
  1221.5 132.1 %copy-start.82 = (f32[32,16]{0,1:T(8,128)S(1)}, f32[32,16]{0,1:T(8,128)}, u32[]{:S(2)}) copy-start(f32[32,16]{0,1:T(8,128)} %param.58) | copy-start | bytes 6148
  1231.0 129.7 %copy-start.84 = (f32[2,32]{1,0:T(2,128)S(1)}, f32[2,32]{1,0:T(2,128)}, u32[]{:S(2)}) copy-start(f32[2,32]{1,0:T(2,128)} %param.45) | copy-start | bytes 772
  1231.0 134.0 %copy-start.57 = (f32[32,1024]{1,0:T(8,128)S(1)}, f32[32,1024]{1,0:T(8,128)}, u32[]{:S(2)}) copy-start(f32[32,1024]{1,0:T(8,128)} %param.48) | copy-start | bytes 393220
  1231.0 134.0 %copy-start.58 = (f32[32,1024]{1,0:T(8,128)S(1)}, f32[32,1024]{1,0:T(8,128)}, u32[]{:S(2)}) copy-start(f32[32,1024]{1,0:T(8,128)} %param.51) | copy-start | bytes 393220
  1231.1 123.2 %copy-start.49 = (bf16[2,2,32,2048]{3,2,0,1:T(8,128)(2,1)S(1)}, bf16[2,2,32,2048]{3,2,0,1:T(8,128)(2,1)}, u32[]{:S(2)}) copy-start(bf16[2,2,32,2048]{3,2,0,1:T(8,128)(2,1)} %copy-done.48) | copy-start | bytes 1572868
  1231.1 123.2 %collective-permute-start.20 = (bf16[2,32,2048]{2,1,0:T(8,128)(2,1)S(1)}, bf16[2,32,2048]{2,1,0:T(8,128)(2,1)}, u32[]{:S(2)}, u32[]{:S(2)}) collective-permute-start(bf16[2,32,2048]{2,1,0:T(8,128)(2,1)S(1)} %dynamic-slice_bitcast_fusion.19), channel_id=1, source_target_pairs={{0,4},{1,5},{2,6},{3,7},{4,0},{5,1},{6,2},{7,3},{8,12},{9,13},{10,... | collective-permute-start | bytes 786440 | tf_op jit(solution)/shard_map/ppermute | solution.py:181
  1233.7 133.5 %copy-start.1 = (s32[2,1,1536,8]{2,3,1,0:T(8,128)S(1)}, s32[2,1,1536,8]{2,3,1,0:T(8,128)}, u32[]{:S(2)}) copy-start(s32[2,1,1536,8]{2,3,1,0:T(8,128)} %param.43) | copy-start | bytes 294916
  1355.3 9.7 collective-permute-start.21
  (67 other events, 345.8 us)
Sparse Core Ops, SparseCore 0:
  12.6 71.4 all-gather.4
  87.7 112.2 all-gather.6
  203.3 92.9 all-gather.8
  299.6 191.8 all-gather.10
  1221.6 130.3 reduce-scatter.3
